TPU v7x, 32 devices: a whole 2x2x4 slice. The times are simulated.
32 devices in a mesh: section: 4 (over y, x), dp: 2 (over core), tensor: 4 (over z).
Axes of the slice: x: 2, y: 2, z: 4, core: 2. Of those that a mesh axis runs over, the one named last changes fastest.
Arguments:
- queries: bfloat16 [1024, 2048], P(('section', 'dp'), 'tensor'), may hold values from -6 to 6
- images: bfloat16 [2, 800, 8192], P('dp', 'section', 'tensor'), may hold values from -6 to 6
- kv_weight: bfloat16 [2, 8192, 256], P(None, 'tensor', 'dp'), may hold values from -0.0625 to 0.0625
- q_gain: float32 [128], replicated, may hold values from 1 to 10
- k_gain: float32 [128], replicated, may hold values from 0.1 to 1.9
- tile_mask: int32 [1024, 4], P(('section', 'dp')), may hold values 0 or 1
Outputs:
- context: bfloat16 [1024, 2048], P(('section', 'dp'), 'tensor')
All inputs are finite; a program needn't handle non-finite values. No bound on the sum of `tile_mask` on one device may be relied on, other than what follows from the above.
Results may differ from a plain program's by a relative error of at most 0.04.
Values may be sent and summed in bfloat16 or wider, within the bound.
No kernel may reach another device: no remote copies, remote signals or barrier semaphores. Data moves between devices by JAX's collectives and lax.ppermute only.
A program may use at most 64 MiB of HBM per device.

v0:
```python
import jax
import jax.numpy as jnp
from jax import lax
from jax.sharding import PartitionSpec as P

EPSILON = 1e-05
MASKED_SCORE = -1e30


def normalize(values, gain_vec):
    mean_sq = jnp.mean(values * values, axis=-1, keepdims=True)
    return values * lax.rsqrt(mean_sq + EPSILON) * gain_vec


def on_device(queries, images, kv_weight, q_gain, k_gain, tile_mask):
    n_section = lax.axis_size("section")
    head_dim = q_gain.shape[0]
    token_count = queries.shape[0]
    head_count = queries.shape[1] // head_dim
    tile_count = tile_mask.shape[1]
    image_rows = images.shape[1]
    features = images[0]
    weight_full = lax.all_gather(kv_weight, "dp", axis=2, tiled=True)
    groups = jnp.arange(1 * lax.axis_size("tensor"), dtype=jnp.int32)
    key_part = jnp.dot(features, weight_full[0], preferred_element_type=jnp.float32)
    value_part = jnp.dot(features, weight_full[1], preferred_element_type=jnp.float32)
    key_units = jnp.transpose(key_part.reshape(image_rows, -1, head_dim), (1, 0, 2))
    value_units = jnp.transpose(value_part.reshape(image_rows, -1, head_dim), (1, 0, 2))
    joined = jnp.concatenate([key_units, value_units], axis=2)
    summed = lax.psum_scatter(
        jnp.take(joined, groups // 2, axis=0).astype(jnp.bfloat16),
        "tensor",
        scatter_dimension=0,
        tiled=True,
    ).astype(jnp.float32)[0]
    key_raw = summed[:, :head_dim]
    value_raw = summed[:, head_dim:]
    key_rows = normalize(key_raw, k_gain).astype(jnp.bfloat16)
    value_rows = value_raw.astype(jnp.bfloat16)
    tile_len = image_rows * n_section // tile_count
    query_rows = queries.reshape(token_count, head_count, head_dim).astype(jnp.float32)
    q_normed = (normalize(query_rows, q_gain) * head_dim ** (-0.5)).astype(jnp.bfloat16)
    mask_float = tile_mask.astype(jnp.float32)
    row_max = jnp.full((head_count, token_count), MASKED_SCORE, jnp.float32)
    key_piece = lax.all_gather(key_rows, "section", axis=0, tiled=True)
    value_piece = lax.all_gather(value_rows, "section", axis=0, tiled=True)
    length = key_piece.shape[0]
    tiles_of = jnp.arange(length, dtype=jnp.int32) // tile_len
    onehot = (tiles_of[:, None] == jnp.arange(tile_count, dtype=jnp.int32)[None, :]).astype(
        jnp.float32
    )
    hidden_bias = jnp.where(jnp.dot(mask_float, onehot.T) > 0.5, 0.0, MASKED_SCORE)
    scores = (
        jnp.einsum("thd,nd->htn", q_normed, key_piece, preferred_element_type=jnp.float32)
        + hidden_bias[None]
    )
    new_max = jnp.maximum(row_max, jnp.max(scores, axis=2))
    weights = jnp.exp(scores - new_max[:, :, None])
    row_sum = jnp.sum(weights, axis=2)
    added = jnp.einsum(
        "htn,nd->htd", weights.astype(jnp.bfloat16), value_piece, preferred_element_type=jnp.float32
    )
    accumulated = added
    row_max, row_sum, accumulated = (new_max, row_sum, accumulated)
    has_any = jnp.sum(mask_float, axis=1) > 0.5
    divided = accumulated / jnp.where(has_any[None, :], row_sum, 1.0)[:, :, None]
    context = jnp.where(has_any[None, :, None], divided, 0.0)
    return (
        jnp.transpose(context, (1, 0, 2))
        .reshape(token_count, head_count * head_dim)
        .astype(jnp.bfloat16)
    )


def solution(mesh):
    in_specs = (
        P(("section", "dp"), "tensor"),
        P("dp", "section", "tensor"),
        P(None, "tensor", "dp"),
        P(),
        P(),
        P(("section", "dp"), None),
    )
    out_specs = P(("section", "dp"), "tensor")
    return jax.shard_map(
        on_device, mesh=mesh, in_specs=in_specs, out_specs=out_specs, check_vma=False
    )
```

profile of v0, /device:TPU:0, one launch (start us, length us, event | category | flops | bytes accessed | tf_op | source)
XLA Modules:
  0.0 80.5 jit_solution(7729440259738522148)
XLA Ops:
  6.5 0.0 copy-start
  6.5 0.0 all-gather.2.cloned.1.call-start
  6.5 0.7 all-gather.2.cloned.1.call-update
  7.3 0.0 reduce-scatter.2.cloned.1.call-start
  7.3 1.0 %reshape.113 = f32[128,4,128]{2,1,0:T(4,128)S(1)} reshape(bf16[128,512]{1,0:T(8,128)(2,1)} %param.6) | data formatting | bytes 393216 | tf_op jit(solution)/shard_map/convert_element_type | solution.py:41
  8.3 0.7 convert_reduce_fusion
  9.1 12.9 %all-gather.2.cloned.1.call-done = bf16[2,2048,256]{2,1,0:T(8,128)(2,1)} async-done(((bf16[2,2048,128]{2,1,0:T(8,128)(2,1)}), bf16[2,2048,256]{2,1,0:T(8,128)(2,1)}) %all-gather.2.cloned.1.call-update) | async-done | bytes 2097168 | tf_op jit(solution)/shard_map/all_gather | solution.py:23
  21.9 2.7 %slice_bitcast_fusion.1 = (bf16[256,2048]{0,1:T(8,128)(2,1)S(1)}, bf16[256,2048]{0,1:T(8,128)(2,1)}) fusion(bf16[2,2048,256]{2,1,0:T(8,128)(2,1)} %all-gather.2.cloned.1.call-done), kind=kLoop, calls=%fused_computation.16 | loop fusion | bytes 4194304 | tf_op jit(solution)/shard_map/dot_general | solution.py:25
  24.6 0.6 copy.15
  25.3 1.5 %copy.16 = bf16[256,2048]{1,0:T(8,128)(2,1)S(1)} copy(bf16[256,2048]{0,1:T(8,128)(2,1)} %get-tuple-element.6) | data formatting | bytes 2097152 | tf_op jit(solution)/shard_map/dot_general | solution.py:26
  26.7 0.0 copy-done
  26.8 0.5 convolution_bitcast_fusion.2
  27.3 0.5 convolution_bitcast_fusion.1
  27.8 0.0 copy-start.1
  27.8 0.0 copy-start.3
  27.8 0.6 gather_fusion
  28.4 0.0 copy-start.2
  28.4 0.9 %select_convert_fusion = bf16[4,200,256]{2,1,0:T(8,128)(2,1)} fusion(bf16[4,200,256]{2,1,0:T(8,128)(2,1)S(1)} %gather_fusion, pred[4]{0:T(512)(128)(4,1)S(1)} %compare_and_fusion), kind=kLoop, calls=%fused_computation.21 | loop fusion | flops 204800 | bytes 819204 | tf_op jit(solution)/shard_map/convert_element_type | solution.py:31
  29.4 0.0 reduce-scatter.2.cloned.1.call-update
  29.4 0.2 multiply_reduce_fusion
  29.6 0.0 copy-done.1
  29.6 0.3 fusion.6
  29.9 0.0 copy-done.3
  29.9 0.2 multiply_convert_fusion
  30.2 21.4 %reduce-scatter.2.cloned.1.call-done = bf16[1,200,256]{2,1,0:T(8,128)(2,1)} async-done(((bf16[4,200,256]{2,1,0:T(8,128)(2,1)}), bf16[1,200,256]{2,1,0:T(8,128)(2,1)}) %reduce-scatter.2.cloned.1.call-update) | async-done | bytes 102416 | tf_op jit(solution)/shard_map/reduce_scatter | solution.py:30
  51.6 0.9 %fusion.18 = f32[200]{0:T(256)S(1)} fusion(bf16[200,256]{1,0:T(8,128)(2,1)} %bitcast.59), kind=kLoop, calls=%fused_computation.33 | loop fusion | flops 76600 | bytes 52000 | tf_op jit(solution)/shard_map/reduce_sum | solution.py:11
  52.5 0.8 %slice.26 = bf16[200,128]{1,0:T(8,128)(2,1)S(1)} slice(bf16[200,256]{1,0:T(8,128)(2,1)} %bitcast.60), slice={[0:200], [128:256]} | slice | bytes 102400 | tf_op jit(solution)/shard_map/slice | solution.py:37
  53.3 8.8 %all_gather.11 = bf16[800,128]{1,0:T(8,128)(2,1)S(1)} all-gather(bf16[200,128]{1,0:T(8,128)(2,1)S(1)} %slice.26), channel_id=1, replica_groups=mesh['section'=4,'dp'=2,'tensor'=4] {'section'}, dimensions={0}, use_global_device_ids=true | all-gather | bytes 256000 | tf_op jit(solution)/shard_map/all_gather | solution.py:46
  62.1 0.0 copy-done.2
  62.1 0.9 %fusion.20 = bf16[200,128]{1,0:T(8,128)(2,1)S(1)} fusion(f32[128]{0:T(128)S(1)} %copy-done.2, f32[200]{0:T(256)S(1)} %add_rsqrt_fusion.1, bf16[200,256]{1,0:T(8,128)(2,1)} %bitcast.61), kind=kLoop, calls=%fused_computation.35 | loop fusion | flops 102400 | bytes 103712 | tf_op jit(solution)/shard_map/convert_element_type | solution.py:38
  63.0 8.7 %all_gather.10 = bf16[800,128]{1,0:T(8,128)(2,1)S(1)} all-gather(bf16[200,128]{1,0:T(8,128)(2,1)S(1)} %fusion.20), channel_id=1, replica_groups=mesh['section'=4,'dp'=2,'tensor'=4] {'section'}, dimensions={0}, use_global_device_ids=true | all-gather | bytes 256000 | tf_op jit(solution)/shard_map/all_gather | solution.py:45
  71.7 0.4 fusion
  72.1 0.3 fusion.1
  72.4 0.5 fusion.7
  72.9 0.8 copy.20
  (10 shorter events, 0.1 us)
Async XLA Ops:
  6.5 20.2 %copy-start = (bf16[1,200,2048]{2,1,0:T(8,128)(2,1)S(1)}, bf16[1,200,2048]{2,1,0:T(8,128)(2,1)}, u32[]{:S(2)}) copy-start(bf16[1,200,2048]{2,1,0:T(8,128)(2,1)} %param.7) | copy-start | bytes 2457604
  6.5 15.4 %all-gather.2.cloned.1.call-start = ((), (), s32[]{:S(2)}) async-start(), calls=%async_computation.1 | async-start | bytes 3145728 | tf_op jit(solution)/shard_map/all_gather | solution.py:23
  7.3 44.3 %reduce-scatter.2.cloned.1.call-start = ((), (), s32[]{:S(2)}) async-start(), calls=%async_computation.2 | async-start | bytes 512000 | tf_op jit(solution)/shard_map/reduce_scatter | solution.py:30
  27.8 1.8 %copy-start.1 = (s32[128,4]{0,1:T(4,128)S(1)}, s32[128,4]{0,1:T(4,128)}, u32[]{:S(2)}) copy-start(s32[128,4]{0,1:T(4,128)} %param.11) | copy-start | bytes 6148
  27.8 2.1 %copy-start.3 = (f32[128]{0:T(128)S(1)}, f32[128]{0:T(128)}, u32[]{:S(2)}) copy-start(f32[128]{0:T(128)} %param.9) | copy-start | bytes 1540
  28.4 33.7 %copy-start.2 = (f32[128]{0:T(128)S(1)}, f32[128]{0:T(128)}, u32[]{:S(2)}) copy-start(f32[128]{0:T(128)} %param.10) | copy-start | bytes 1540
Sparse Core Ops, SparseCore 0:
  8.9 13.0 all-gather.1
  29.5 21.9 reduce-scatter.1
where the time goes:
time: 80.9 us; the launch traced here: 80.5 us
  waiting for transfers between devices  35 us (43%)
  blocking collectives  17.5 us (22%)
  between operations  13.6 us (17%)
  local copies, waits for them, and re-layouts  7.95 us (10%)
  other arithmetic  4.23 us (5%)
  matrix products  2.16 us (3%)
    reduce_scatter x1, waiting for transfers between devices, on_device(): lax.psum_scatter(jnp.take(joined, groups // 2, axis=0).astype(jnp.bfloat1...  21.4 us
    all_gather x1, waiting for transfers between devices, on_device(): weight_full = lax.all_gather(kv_weight, 'dp', axis=2, tiled=True)  12.9 us
    all_gather x1, blocking collectives, on_device(): value_piece = lax.all_gather(value_rows, 'section', axis=0, tiled=True)  8.79 us
    all_gather x1, blocking collectives, on_device(): key_piece = lax.all_gather(key_rows, 'section', axis=0, tiled=True)  8.71 us
    dot_general x2, local copies, waits for them, and re-layouts, on_device(): jnp.dot(features, weight_full[0], preferred_element_type=jnp.float32)  3.29 us
  transfers between devices with their start and end apart: 2, of which 2 were waited for; matrix products, arithmetic and copies ran while one was open for 3% of the time, Pallas kernels for 0%

commit v1 on v0

v1 whole, which is shorter than its diff:
```python
import functools

import jax
import jax.numpy as jnp
from jax import lax
from jax.experimental import pallas as pl
from jax.experimental.pallas import tpu as pltpu
from jax.sharding import PartitionSpec as P

EPSILON = 1e-05
MASKED_SCORE = -1e30
TOP_FLOOR = -1e29
VMEM = pl.BlockSpec(memory_space=pltpu.VMEM)
HBM = pl.BlockSpec(memory_space=pltpu.HBM)
F32 = jnp.float32
MIB = 1024 * 1024
LIMIT = 24 * MIB
BF16 = jnp.bfloat16


def shape_of(dims, dtype=BF16):
    return jax.ShapeDtypeStruct(dims, dtype)


def call(
    kernel, outs, n_in, name, flops=0, size=0, exps=0, in_specs=None, scratch=()
):
    many = isinstance(outs, list)
    return pl.pallas_call(
        kernel,
        out_shape=outs,
        in_specs=in_specs or [VMEM] * n_in,
        out_specs=[VMEM] * len(outs) if many else VMEM,
        scratch_shapes=scratch,
        compiler_params=pltpu.CompilerParams(vmem_limit_bytes=LIMIT),
        cost_estimate=pl.CostEstimate(flops=flops, bytes_accessed=size, transcendentals=exps),
        name=name,
    )


def normalize(values, gain_vec):
    mean_sq = jnp.mean(values * values, axis=-1, keepdims=True)
    return values * lax.rsqrt(mean_sq + EPSILON) * gain_vec


def project(x, w):
    return jnp.dot(
        x, jnp.concatenate([w[0], w[1]], axis=1), preferred_element_type=F32
    ).astype(BF16)


def store_heads(ref, base, both, head_dim):
    width = both.shape[1] // 2
    for head in range(width // head_dim):
        lo = head * head_dim
        ref[base + head, 0] = both[:, lo : lo + head_dim]
        ref[base + head, 1] = both[:, width + lo : width + lo + head_dim]


def own_kernel(
    head_dim, x_hbm, w_hbm, q_hbm, q_gain_hbm, k_gain_hbm, mask_hbm,
    own_ref, x_ref, k_gain_ref, qt_ref, bias_ref,
    w_ref, q_ref, q_gain_ref, mask_ref, sems,
):
    moves = [
        (q_hbm, q_ref),
        (q_gain_hbm, q_gain_ref),
        (mask_hbm, mask_ref),
        (k_gain_hbm, k_gain_ref),
        (x_hbm, x_ref),
        (w_hbm, w_ref),
    ]
    copies = [pltpu.make_async_copy(a, b, sems.at[i]) for i, (a, b) in enumerate(moves)]
    for copy in copies:
        copy.start()
    for copy in copies[:4]:
        copy.wait()
    tokens = q_ref.shape[0]
    bias = jnp.where(mask_ref[...] > 0, 0.0, MASKED_SCORE).astype(F32)
    for head in range(q_ref.shape[1] // head_dim):
        rows = q_ref[:, head * head_dim : (head + 1) * head_dim].astype(F32)
        normed = normalize(rows, q_gain_ref[...]) * head_dim ** (-0.5)
        qt_ref[:, head * tokens : (head + 1) * tokens] = normed.T.astype(BF16)
        bias_ref[:, head * tokens : (head + 1) * tokens] = bias
    for copy in copies[4:]:
        copy.wait()
    store_heads(own_ref, 0, project(x_ref[0], w_ref[...]), head_dim)


def split_half(held, send_ref, keep_ref, partner_heads, own_heads):
    for i in range(send_ref.shape[0]):
        send_ref[i] = held[partner_heads + i]
        keep_ref[i] = held[own_heads + i]


def other_kernel(head_dim, n_dp, n_tensor, x_ref, own_ref, *refs):
    w_refs = refs[: n_dp - 1]
    send_ref, keep_ref, held = refs[n_dp - 1 :]
    d = lax.axis_index("dp")
    t = lax.axis_index("tensor")
    own_heads = own_ref.shape[0]
    held[pl.ds(d * own_heads, own_heads)] = own_ref[...]
    for k in range(1, n_dp):
        store_heads(held, (d ^ k) * own_heads, project(x_ref[0], w_refs[k - 1][...]), head_dim)
    half = send_ref.shape[0]
    upper = t // (n_tensor // 2)
    split_half(held, send_ref, keep_ref, (1 - upper) * half, upper * half)


def add_kernel(bit, keep_ref, arrived_ref, send_ref, next_ref, held):
    held[...] = (keep_ref[...].astype(F32) + arrived_ref[...].astype(F32)).astype(BF16)
    half = send_ref.shape[0]
    upper = (lax.axis_index("tensor") // bit) % 2
    split_half(held, send_ref, next_ref, (1 - upper) * half, upper * half)


def add_last_kernel(keep_ref, arrived_ref, out_ref):
    out_ref[...] = (keep_ref[...].astype(F32) + arrived_ref[...].astype(F32)).astype(BF16)


def norm_kernel(k_gain_ref, keep_ref, arrived_ref, kv_ref):
    total = keep_ref[0].astype(F32) + arrived_ref[0].astype(F32)
    kv_ref[0] = normalize(total[0], k_gain_ref[...]).astype(BF16)
    kv_ref[1] = total[1].astype(BF16)


def attend_kernel(steps, tile_len, first, last, head_dim, qt_ref, bias_ref, *refs):
    parts, refs = refs[: len(steps)], refs[len(steps) :]
    if not first:
        top_in, sum_in, mixed_in = refs[:3]
        refs = refs[3:]
    s = lax.axis_index("section")
    rows = parts[0].shape[1]
    qt = qt_ref[...]
    scores, biases = [], []
    top = TOP_FLOOR if first else top_in[...]
    for k, part in zip(steps, parts):
        score = jnp.dot(part[0], qt, preferred_element_type=F32)
        bias = bias_ref[pl.ds(((s ^ k) * rows) // tile_len, 1), :]
        scores.append(score)
        biases.append(bias)
        top = jnp.maximum(top, jnp.max(score, axis=0, keepdims=True) + bias)
    row_sum, mixed = 0.0, 0.0
    if not first:
        scale = jnp.exp(top_in[...] - top)
        row_sum = sum_in[...] * scale
        mixed = mixed_in[...] * scale
    for part, score, bias in zip(parts, scores, biases):
        weights = jnp.exp(score + (bias - top))
        row_sum = row_sum + jnp.sum(weights, axis=0, keepdims=True)
        mixed = mixed + lax.dot_general(
            part[1], weights.astype(BF16), (((0,), (0,)), ((), ())), preferred_element_type=F32
        )
    if not last:
        top_out, sum_out, mixed_out = refs
        top_out[...] = top
        sum_out[...] = row_sum
        mixed_out[...] = mixed
        return
    (out,) = refs
    has_any = jnp.max(bias_ref[...], axis=0, keepdims=True) > -1.0
    context = jnp.where(has_any, mixed / jnp.where(has_any, row_sum, 1.0), 0.0)
    tokens = out.shape[0]
    for head in range(out.shape[1] // head_dim):
        out[:, head * head_dim : (head + 1) * head_dim] = context[
            :, head * tokens : (head + 1) * tokens
        ].T.astype(BF16)


def on_device(queries, images, kv_weight, q_gain, k_gain, tile_mask):
    n_section = lax.axis_size("section")
    n_dp = lax.axis_size("dp")
    n_tensor = lax.axis_size("tensor")
    head_dim = q_gain.shape[0]
    tokens, q_width = queries.shape
    rows, features = images.shape[1:]
    tiles = tile_mask.shape[1]
    own_heads = kv_weight.shape[2] // head_dim
    heads = own_heads * n_dp
    tile_len = rows * n_section // tiles
    assert heads * 2 == n_tensor and tile_len % rows == 0
    pairs = tokens * (q_width // head_dim)
    work = 4 * rows * features * kv_weight.shape[2]

    def swap(value, axis, k):
        return lax.ppermute(value, axis, [(i, i ^ k) for i in range(lax.axis_size(axis))])

    others = [swap(kv_weight, "dp", k) for k in range(1, n_dp)]
    own, x, gain, qt, bias = call(
        functools.partial(own_kernel, head_dim),
        [
            shape_of((own_heads, 2, rows, head_dim)),
            shape_of(images.shape),
            shape_of((1, head_dim), F32),
            shape_of((head_dim, pairs)),
            shape_of((tiles, pairs), F32),
        ],
        6,
        "own_head",
        flops=work,
        size=2 * (images.size + kv_weight.size),
        in_specs=[HBM] * 6,
        scratch=[
            pltpu.VMEM(kv_weight.shape, BF16),
            pltpu.VMEM(queries.shape, BF16),
            pltpu.VMEM((1, head_dim), F32),
            pltpu.VMEM((tiles, tokens), jnp.int32),
            pltpu.SemaphoreType.DMA((6,)),
        ],
    )(
        *[
            pltpu.with_memory_space_constraint(value, pltpu.HBM)
            for value in (
                images, kv_weight, queries, q_gain.reshape(1, -1), k_gain.reshape(1, -1), tile_mask.T,
            )
        ]
    )
    half = shape_of((heads // 2, 2, rows, head_dim))
    send, keep = call(
        functools.partial(other_kernel, head_dim, n_dp, n_tensor),
        [half, half],
        n_dp + 1,
        "other_heads",
        flops=work * (n_dp - 1),
        scratch=[pltpu.VMEM((heads, 2, rows, head_dim), BF16)],
    )(x, own, *others)
    bit = n_tensor // 2
    while bit > 1:
        arrived = swap(send, "tensor", bit)
        bit //= 2
        now = keep.shape
        if bit > 1:
            half = shape_of((now[0] // 2, *now[1:]))
            send, keep = call(
                functools.partial(add_kernel, bit),
                [half, half],
                2,
                "add_part",
                scratch=[pltpu.VMEM(now, BF16)],
            )(keep, arrived)
        else:
            send = keep = call(add_last_kernel, shape_of(now), 2, "add_pair")(keep, arrived)
    arrived = swap(send, "tensor", 1)
    kv = call(norm_kernel, shape_of((2, rows, head_dim)), 3, "sum_norm")(gain, keep, arrived)

    gathered = [kv] + [swap(kv, "section", k) for k in range(1, n_section)]
    state = []
    for steps in ([0], list(range(1, n_section - 1)), [n_section - 1]):
        first, last = steps[0] == 0, steps[-1] == n_section - 1
        outs = (
            shape_of((tokens, q_width))
            if last
            else [shape_of((1, pairs), F32), shape_of((1, pairs), F32), shape_of((head_dim, pairs), F32)]
        )
        state = call(
            functools.partial(attend_kernel, steps, tile_len, first, last, head_dim),
            outs,
            2 + len(steps) + len(state),
            "attend",
            flops=4 * pairs * rows * head_dim * len(steps),
            exps=pairs * rows * len(steps),
        )(qt, bias, *[gathered[k] for k in steps], *state)
    return state


def solution(mesh):
    in_specs = (
        P(("section", "dp"), "tensor"),
        P("dp", "section", "tensor"),
        P(None, "tensor", "dp"),
        P(),
        P(),
        P(("section", "dp"), None),
    )
    out_specs = P(("section", "dp"), "tensor")
    return jax.shard_map(
        on_device, mesh=mesh, in_specs=in_specs, out_specs=out_specs, check_vma=False
    )
```

time: 80.9 us -> 27.7 us (0.34)
  waiting for transfers between devices: 35 us -> 13.9 us
  blocking collectives: 17.5 us -> 0 us
  between operations: 13.6 us -> 0.05 us
  starting transfers between devices: 0.04 us -> 8.81 us
  local copies, waits for them, and re-layouts: 7.95 us -> 0 us
  Pallas kernels: 0 us -> 4.8 us
  other arithmetic: 4.23 us -> 0 us
  matrix products: 2.16 us -> 0 us
    reduce_scatter x1 -> x0, waiting for transfers between devices: 21.4 us -> none  [on_device(): lax.psum_scatter(jnp.take(joined, groups // 2, axis=0).astype(jnp.bfloat1...]
    all_gather x2 -> x0, blocking collectives: 17.5 us -> none  [the longest x1 8.79 us: on_device(): value_piece = lax.all_gather(value_rows, 'section', axis=0, tiled=True)]
    ppermute x0 -> x6, waiting for transfers between devices: none -> 13.9 us  [swap(): lax.ppermute(value, axis, [(i, i ^ k) for i in range(lax.axis_size(axis))])]
    all_gather x1 -> x0, waiting for transfers between devices: 12.9 us -> none  [on_device(): weight_full = lax.all_gather(kv_weight, 'dp', axis=2, tiled=True)]
    ppermute x0 -> x6, starting transfers between devices: none -> 8.81 us  [swap(): lax.ppermute(value, axis, [(i, i ^ k) for i in range(lax.axis_size(axis))])]
    pallas_call x0 -> x7, Pallas kernels: none -> 4.8 us  [the longest x3 2.18 us: on_device(): call(functools.partial(attend_kernel, steps, tile_len, first, last, head_...]
    dot_general x3 -> x0, local copies, waits for them, and re-layouts: 4.78 us -> none  [the longest x2 3.29 us: on_device(): jnp.dot(features, weight_full[0], preferred_element_type=jnp.float32)]
    dot_general x5 -> x0, matrix products: 2.16 us -> none  [the longest x1 0.51 us: on_device(): jnp.dot(features, weight_full[0], preferred_element_type=jnp.float32)]
  transfers between devices with their start and end apart: 2 -> 6, of which waited for: 2 -> 6; matrix products, arithmetic and copies ran while one was open for 3% -> 0% of each run, Pallas kernels for 0% -> 11%
where the time goes in v1:
time: 27.7 us; the launch traced here: 27.5 us
  waiting for transfers between devices  13.9 us (50%)
  starting transfers between devices  8.81 us (32%)
  Pallas kernels  4.8 us (17%)
    ppermute x6, waiting for transfers between devices, swap(): lax.ppermute(value, axis, [(i, i ^ k) for i in range(lax.axis_size(axis))])  13.9 us
    ppermute x6, starting transfers between devices, swap(): lax.ppermute(value, axis, [(i, i ^ k) for i in range(lax.axis_size(axis))])  8.81 us
    pallas_call x3, Pallas kernels, on_device(): call(functools.partial(attend_kernel, steps, tile_len, first, last, head_...  2.18 us
    pallas_call x1, Pallas kernels, on_device(): call(functools.partial(own_kernel, head_dim), [shape_of((own_heads, 2, ro...  2.05 us
  transfers between devices with their start and end apart: 6, of which 6 were waited for; matrix products, arithmetic and copies ran while one was open for 0% of the time, Pallas kernels for 11%

profile of v1, /device:TPU:0, one launch (start us, length us, event | category | flops | bytes accessed | tf_op | source)
XLA Modules:
  0.0 27.5 jit_solution(16316188916186351182)
XLA Ops:
  0.0 0.5 %collective-permute-start = (bf16[2,2048,128]{2,1,0:T(8,128)(2,1)}, bf16[2,2048,128]{2,1,0:T(8,128)(2,1)S(1)}, u32[]{:S(2)}, u32[]{:S(2)}) collective-permute-start(bf16[2,2048,128]{2,1,0:T(8,128)(2,1)} %w_hbm.1), channel_id=1, source_target_pairs={{0,4},{4,0},{1,5},{5,1},{2,6},{6,2},{3,7},{7,3},{8,12},{12,8},{9,1... | collective-permute-start | bytes 3145736 | tf_op jit(solution)/shard_map/ppermute | solution.py:186
  0.5 2.1 %own_head.1 = (bf16[1,2,200,128]{3,2,1,0:T(8,128)(2,1)S(1)}, bf16[1,200,2048]{2,1,0:T(8,128)(2,1)S(1)}, f32[1,128]{1,0:T(1,128)S(1)}, bf16[128,512]{1,0:T(8,128)(2,1)S(1)}, f32[4,512]{1,0:T(4,128)S(1)}) custom-call(bf16[1,200,2048]{2,1,0:T(8,128)(2,1)} %x_hbm.1, bf16[2,2048,128]{2,1,0:T(8,128)(2,1)} %w_hbm.1, bf16[128,512]{1,0:T(8,128)(2,1)} %q_hbm.1, ...), custom_call_target="tpu_custom_call" | custom-call | flops 209715200 | bytes 1867776 | tf_op jit(solution)/shard_map/own_head/pallas_call | solution.py:189
  2.5 0.4 %collective-permute-done.refs_0_ = bf16[2,2048,128]{2,1,0:T(8,128)(2,1)S(1)} collective-permute-done((bf16[2,2048,128]{2,1,0:T(8,128)(2,1)}, bf16[2,2048,128]{2,1,0:T(8,128)(2,1)S(1)}, u32[]{:S(2)}, u32[]{:S(2)}) %collective-permute-start) | collective-permute-done | bytes 1048608 | tf_op jit(solution)/shard_map/ppermute | solution.py:186
  3.0 0.4 %other_heads.1 = (bf16[1,2,200,128]{3,2,1,0:T(8,128)(2,1)S(1)}, bf16[1,2,200,128]{3,2,1,0:T(8,128)(2,1)S(1)}) custom-call(bf16[1,200,2048]{2,1,0:T(8,128)(2,1)S(1)} %get-tuple-element.21.x_ref, bf16[1,2,200,128]{3,2,1,0:T(8,128)(2,1)S(1)} %get-tuple-element.22.own_ref, bf16[2,2048,128]{2,1,0:T(8,128)(2,1)S(1)} %collective-permute-done.refs_0_), custom_call_target="tpu_custom_call" | custom-call | flops 209715200 | tf_op jit(solution)/shard_map/other_heads/pallas_call | solution.py:219
  3.4 4.0 %collective-permute-start.1 = (bf16[1,2,200,128]{3,2,1,0:T(8,128)(2,1)S(1)}, bf16[1,2,200,128]{3,2,1,0:T(8,128)(2,1)S(1)}, u32[]{:S(2)}, u32[]{:S(2)}) collective-permute-start(bf16[1,2,200,128]{3,2,1,0:T(8,128)(2,1)S(1)} %get-tuple-element.24), channel_id=1, source_target_pairs={{0,2},{1,3},{2,0},{3,1},{4,6},{5,7},{6,4},{7,5},{8,10},{9,11},{10,... | collective-permute-start | bytes 307208 | tf_op jit(solution)/shard_map/ppermute | solution.py:186
  7.4 5.4 %collective-permute-done.1.arrived_ref = bf16[1,2,200,128]{3,2,1,0:T(8,128)(2,1)S(1)} collective-permute-done((bf16[1,2,200,128]{3,2,1,0:T(8,128)(2,1)S(1)}, bf16[1,2,200,128]{3,2,1,0:T(8,128)(2,1)S(1)}, u32[]{:S(2)}, u32[]{:S(2)}) %collective-permute-start.1) | collective-permute-done | bytes 102432 | tf_op jit(solution)/shard_map/ppermute | solution.py:186
  12.8 0.8 %collective-permute-start.2 = (bf16[1,2,200,128]{3,2,1,0:T(8,128)(2,1)S(1)}, bf16[1,2,200,128]{3,2,1,0:T(8,128)(2,1)S(1)}, u32[]{:S(2)}, u32[]{:S(2)}) collective-permute-start(bf16[1,2,200,128]{3,2,1,0:T(8,128)(2,1)S(1)} %add_pair.1.keep_ref), channel_id=1, source_target_pairs={{0,1},{1,0},{2,3},{3,2},{4,5},{5,4},{6,7},{7,6},{8,9},{9,8},{10,11... | collective-permute-start | bytes 307208 | tf_op jit(solution)/shard_map/ppermute | solution.py:186
  13.6 3.9 %collective-permute-done.2.arrived_ref = bf16[1,2,200,128]{3,2,1,0:T(8,128)(2,1)S(1)} collective-permute-done((bf16[1,2,200,128]{3,2,1,0:T(8,128)(2,1)S(1)}, bf16[1,2,200,128]{3,2,1,0:T(8,128)(2,1)S(1)}, u32[]{:S(2)}, u32[]{:S(2)}) %collective-permute-start.2) | collective-permute-done | bytes 102432 | tf_op jit(solution)/shard_map/ppermute | solution.py:186
  17.5 0.1 sum_norm.1.refs_0_
  17.7 1.6 %collective-permute-start.4 = (bf16[2,200,128]{2,1,0:T(8,128)(2,1)S(1)}, bf16[2,200,128]{2,1,0:T(8,128)(2,1)S(1)}, u32[]{:S(2)}, u32[]{:S(2)}) collective-permute-start(bf16[2,200,128]{2,1,0:T(8,128)(2,1)S(1)} %sum_norm.1.refs_0_), channel_id=1, source_target_pairs={{0,8},{8,0},{16,24},{24,16},{1,9},{9,1},{17,25},{25,17},{2,10},{10... | collective-permute-start | bytes 307208 | tf_op jit(solution)/shard_map/ppermute | solution.py:186
  19.3 1.5 %collective-permute-start.5 = (bf16[2,200,128]{2,1,0:T(8,128)(2,1)S(1)}, bf16[2,200,128]{2,1,0:T(8,128)(2,1)S(1)}, u32[]{:S(2)}, u32[]{:S(2)}) collective-permute-start(bf16[2,200,128]{2,1,0:T(8,128)(2,1)S(1)} %sum_norm.1.refs_0_), channel_id=1, source_target_pairs={{0,16},{8,24},{16,0},{24,8},{1,17},{9,25},{17,1},{25,9},{2,18},{10... | collective-permute-start | bytes 307208 | tf_op jit(solution)/shard_map/ppermute | solution.py:186
  20.8 0.4 %collective-permute-start.3 = (bf16[2,200,128]{2,1,0:T(8,128)(2,1)S(1)}, bf16[2,200,128]{2,1,0:T(8,128)(2,1)S(1)}, u32[]{:S(2)}, u32[]{:S(2)}) collective-permute-start(bf16[2,200,128]{2,1,0:T(8,128)(2,1)S(1)} %sum_norm.1.refs_0_), channel_id=1, source_target_pairs={{0,24},{8,16},{16,8},{24,0},{1,25},{9,17},{17,9},{25,1},{2,26},{10... | collective-permute-start | bytes 307208 | tf_op jit(solution)/shard_map/ppermute | solution.py:186
  21.2 0.4 %attend.3 = (f32[1,512]{1,0:T(1,128)S(1)}, f32[1,512]{1,0:T(1,128)S(1)}, f32[128,512]{1,0:T(8,128)S(1)}) custom-call(bf16[128,512]{1,0:T(8,128)(2,1)S(1)} %get-tuple-element.18.qt_ref, f32[4,512]{1,0:T(4,128)S(1)} %get-tuple-element.19.bias_ref, bf16[2,200,128]{2,1,0:T(8,128)(2,1)S(1)} %sum_norm.1.refs_0_), custom_call_target="tpu_custom_call" | custom-call | flops 52428800 | tf_op jit(solution)/shard_map/attend/pallas_call | solution.py:255
  21.7 1.5 %collective-permute-done.4.refs_0_ = bf16[2,200,128]{2,1,0:T(8,128)(2,1)S(1)} collective-permute-done((bf16[2,200,128]{2,1,0:T(8,128)(2,1)S(1)}, bf16[2,200,128]{2,1,0:T(8,128)(2,1)S(1)}, u32[]{:S(2)}, u32[]{:S(2)}) %collective-permute-start.4) | collective-permute-done | bytes 102432 | tf_op jit(solution)/shard_map/ppermute | solution.py:186
  23.1 1.3 %collective-permute-done.5.refs_1_ = bf16[2,200,128]{2,1,0:T(8,128)(2,1)S(1)} collective-permute-done((bf16[2,200,128]{2,1,0:T(8,128)(2,1)S(1)}, bf16[2,200,128]{2,1,0:T(8,128)(2,1)S(1)}, u32[]{:S(2)}, u32[]{:S(2)}) %collective-permute-start.5) | collective-permute-done | bytes 102432 | tf_op jit(solution)/shard_map/ppermute | solution.py:186
  24.4 0.6 %attend.4 = (f32[1,512]{1,0:T(1,128)S(1)}, f32[1,512]{1,0:T(1,128)S(1)}, f32[128,512]{1,0:T(8,128)S(1)}) custom-call(bf16[128,512]{1,0:T(8,128)(2,1)S(1)} %get-tuple-element.18.qt_ref, f32[4,512]{1,0:T(4,128)S(1)} %get-tuple-element.19.bias_ref, bf16[2,200,128]{2,1,0:T(8,128)(2,1)S(1)} %collective-permute-done.4.refs_0_, ...), custom_call_target="tpu_custom_call" | custom-call | flops 104857600 | tf_op jit(solution)/shard_map/attend/pallas_call | solution.py:255
  25.0 1.4 %collective-permute-done.3.refs_0_ = bf16[2,200,128]{2,1,0:T(8,128)(2,1)S(1)} collective-permute-done((bf16[2,200,128]{2,1,0:T(8,128)(2,1)S(1)}, bf16[2,200,128]{2,1,0:T(8,128)(2,1)S(1)}, u32[]{:S(2)}, u32[]{:S(2)}) %collective-permute-start.3) | collective-permute-done | bytes 102432 | tf_op jit(solution)/shard_map/ppermute | solution.py:186
  26.4 1.2 %attend.5 = bf16[128,512]{1,0:T(8,128)(2,1)} custom-call(bf16[128,512]{1,0:T(8,128)(2,1)S(1)} %get-tuple-element.18.qt_ref, f32[4,512]{1,0:T(4,128)S(1)} %get-tuple-element.19.bias_ref, bf16[2,200,128]{2,1,0:T(8,128)(2,1)S(1)} %collective-permute-done.3.refs_0_, f32[1,512]{1,0:T(1,128)S(1)} %get-tuple-element.28.refs_1_, ...), custom_call_target="tpu_custom_call" | custom-call | flops 52428800 | tf_op jit(solution)/shard_map/attend/pallas_call | solution.py:255
  (1 shorter events, 0.0 us)
Async XLA Ops:
  0.0 3.0 %collective-permute-start = (bf16[2,2048,128]{2,1,0:T(8,128)(2,1)}, bf16[2,2048,128]{2,1,0:T(8,128)(2,1)S(1)}, u32[]{:S(2)}, u32[]{:S(2)}) collective-permute-start(bf16[2,2048,128]{2,1,0:T(8,128)(2,1)} %w_hbm.1), channel_id=1, source_target_pairs={{0,4},{4,0},{1,5},{5,1},{2,6},{6,2},{3,7},{7,3},{8,12},{12,8},{9,1... | collective-permute-start | bytes 3145736 | tf_op jit(solution)/shard_map/ppermute | solution.py:186
  3.4 9.4 %collective-permute-start.1 = (bf16[1,2,200,128]{3,2,1,0:T(8,128)(2,1)S(1)}, bf16[1,2,200,128]{3,2,1,0:T(8,128)(2,1)S(1)}, u32[]{:S(2)}, u32[]{:S(2)}) collective-permute-start(bf16[1,2,200,128]{3,2,1,0:T(8,128)(2,1)S(1)} %get-tuple-element.24), channel_id=1, source_target_pairs={{0,2},{1,3},{2,0},{3,1},{4,6},{5,7},{6,4},{7,5},{8,10},{9,11},{10,... | collective-permute-start | bytes 307208 | tf_op jit(solution)/shard_map/ppermute | solution.py:186
  12.8 4.7 %collective-permute-start.2 = (bf16[1,2,200,128]{3,2,1,0:T(8,128)(2,1)S(1)}, bf16[1,2,200,128]{3,2,1,0:T(8,128)(2,1)S(1)}, u32[]{:S(2)}, u32[]{:S(2)}) collective-permute-start(bf16[1,2,200,128]{3,2,1,0:T(8,128)(2,1)S(1)} %add_pair.1.keep_ref), channel_id=1, source_target_pairs={{0,1},{1,0},{2,3},{3,2},{4,5},{5,4},{6,7},{7,6},{8,9},{9,8},{10,11... | collective-permute-start | bytes 307208 | tf_op jit(solution)/shard_map/ppermute | solution.py:186
  17.7 5.5 %collective-permute-start.4 = (bf16[2,200,128]{2,1,0:T(8,128)(2,1)S(1)}, bf16[2,200,128]{2,1,0:T(8,128)(2,1)S(1)}, u32[]{:S(2)}, u32[]{:S(2)}) collective-permute-start(bf16[2,200,128]{2,1,0:T(8,128)(2,1)S(1)} %sum_norm.1.refs_0_), channel_id=1, source_target_pairs={{0,8},{8,0},{16,24},{24,16},{1,9},{9,1},{17,25},{25,17},{2,10},{10... | collective-permute-start | bytes 307208 | tf_op jit(solution)/shard_map/ppermute | solution.py:186
  19.3 5.1 %collective-permute-start.5 = (bf16[2,200,128]{2,1,0:T(8,128)(2,1)S(1)}, bf16[2,200,128]{2,1,0:T(8,128)(2,1)S(1)}, u32[]{:S(2)}, u32[]{:S(2)}) collective-permute-start(bf16[2,200,128]{2,1,0:T(8,128)(2,1)S(1)} %sum_norm.1.refs_0_), channel_id=1, source_target_pairs={{0,16},{8,24},{16,0},{24,8},{1,17},{9,25},{17,1},{25,9},{2,18},{10... | collective-permute-start | bytes 307208 | tf_op jit(solution)/shard_map/ppermute | solution.py:186
  20.8 5.6 %collective-permute-start.3 = (bf16[2,200,128]{2,1,0:T(8,128)(2,1)S(1)}, bf16[2,200,128]{2,1,0:T(8,128)(2,1)S(1)}, u32[]{:S(2)}, u32[]{:S(2)}) collective-permute-start(bf16[2,200,128]{2,1,0:T(8,128)(2,1)S(1)} %sum_norm.1.refs_0_), channel_id=1, source_target_pairs={{0,24},{8,16},{16,8},{24,0},{1,25},{9,17},{17,9},{25,1},{2,26},{10... | collective-permute-start | bytes 307208 | tf_op jit(solution)/shard_map/ppermute | solution.py:186

commit v2 on v1

v2 whole, which is shorter than its diff:
```python
import functools

import jax
import jax.numpy as jnp
from jax import lax
from jax.experimental import pallas as pl
from jax.experimental.pallas import tpu as pltpu
from jax.sharding import PartitionSpec as P

EPSILON = 1e-05
MASKED_SCORE = -1e30
TOP_FLOOR = -1e29
VMEM = pl.BlockSpec(memory_space=pltpu.VMEM)
HBM = pl.BlockSpec(memory_space=pltpu.HBM)
F32 = jnp.float32
BF16 = jnp.bfloat16
LIMIT = 24 * 1024 * 1024
CHUNKS = 4


def shape_of(dims, dtype=BF16):
    return jax.ShapeDtypeStruct(dims, dtype)


def call(kernel, outs, name, in_specs, flops=0, size=0, exps=0, scratch=()):
    many = isinstance(outs, list)
    return pl.pallas_call(
        kernel,
        out_shape=outs,
        in_specs=in_specs,
        out_specs=[VMEM] * len(outs) if many else VMEM,
        scratch_shapes=scratch,
        compiler_params=pltpu.CompilerParams(vmem_limit_bytes=LIMIT),
        cost_estimate=pl.CostEstimate(flops=flops, bytes_accessed=size, transcendentals=exps),
        name=name,
    )


def in_hbm(*values):
    return [pltpu.with_memory_space_constraint(value, pltpu.HBM) for value in values]


def normalize(values, gain_vec):
    mean_sq = jnp.mean(values * values, axis=-1, keepdims=True)
    return values * lax.rsqrt(mean_sq + EPSILON) * gain_vec


def part_pair(both, send_ref, keep_ref):
    width = both.shape[1] // 2
    both = both.astype(BF16)
    even = lax.axis_index("tensor") % 2 == 0
    for head in range(send_ref.shape[0]):
        lo = head * send_ref.shape[2]
        keys = both[:, lo : lo + send_ref.shape[2]]
        values = both[:, width + lo : width + lo + send_ref.shape[2]]
        send_ref[head] = jnp.where(even, values, keys)
        keep_ref[head] = jnp.where(even, keys, values)


def own_kernel(x_hbm, w_hbm, send_ref, keep_ref, x_ref, w_ref, sems):
    step = x_ref.shape[1] // CHUNKS
    copies = []
    for i in range(CHUNKS):
        cols = pl.ds(i * step, step)
        copies.append(
            (
                pltpu.make_async_copy(w_hbm.at[:, cols], w_ref.at[:, cols], sems.at[0, i]),
                pltpu.make_async_copy(x_hbm.at[0, :, cols], x_ref.at[:, cols], sems.at[1, i]),
            )
        )
        for copy in copies[-1]:
            copy.start()
    both = None
    for i in range(CHUNKS):
        for copy in copies[i]:
            copy.wait()
        cols = slice(i * step, (i + 1) * step)
        part = jnp.dot(
            x_ref[:, cols],
            jnp.concatenate([w_ref[0, cols], w_ref[1, cols]], axis=1),
            preferred_element_type=F32,
        )
        both = part if both is None else both + part
    part_pair(both, send_ref, keep_ref)


def other_kernel(x_ref, w_ref, send_ref, keep_ref):
    both = jnp.dot(
        x_ref[...],
        jnp.concatenate([w_ref[0], w_ref[1]], axis=1),
        preferred_element_type=F32,
    )
    part_pair(both, send_ref, keep_ref)


def query_kernel(
    q_hbm, q_gain_hbm, k_gain_hbm, mask_hbm, qt_ref, bias_ref, k_gain_ref,
    q_ref, q_gain_ref, mask_ref, sems,
):
    moves = [
        (q_hbm, q_ref),
        (q_gain_hbm, q_gain_ref),
        (mask_hbm, mask_ref),
        (k_gain_hbm, k_gain_ref),
    ]
    copies = [pltpu.make_async_copy(a, b, sems.at[i]) for i, (a, b) in enumerate(moves)]
    for copy in copies:
        copy.start()
    for copy in copies:
        copy.wait()
    tokens = q_ref.shape[0]
    head_dim = q_gain_ref.shape[1]
    bias = jnp.where(mask_ref[...] > 0, 0.0, MASKED_SCORE).astype(F32)
    for head in range(q_ref.shape[1] // head_dim):
        rows = q_ref[:, head * head_dim : (head + 1) * head_dim].astype(F32)
        normed = normalize(rows, q_gain_ref[...]) * head_dim ** (-0.5)
        qt_ref[:, head * tokens : (head + 1) * tokens] = normed.T.astype(BF16)
        bias_ref[:, head * tokens : (head + 1) * tokens] = bias


def pair_kernel(k, keep_ref, arrived_ref, mine_ref, *send_refs):
    heads = keep_ref.shape[0]
    pair = lax.axis_index("tensor") // 2
    group = lax.axis_index("dp") ^ k
    own = pair % heads
    total = keep_ref[own].astype(F32) + arrived_ref[own].astype(F32)
    mine_ref[...] = jnp.where(pair // heads == group, total, 0.0)
    for j, ref in enumerate(send_refs, 1):
        head = (pair ^ j) % heads
        ref[...] = (keep_ref[head].astype(F32) + arrived_ref[head].astype(F32)).astype(BF16)


def norm_kernel(k_gain_ref, *refs):
    out = refs[-1]
    total = refs[0][...].astype(F32)
    for ref in refs[1:-1]:
        total = total + ref[...].astype(F32)
    even = lax.axis_index("tensor") % 2 == 0
    out[...] = jnp.where(even, normalize(total, k_gain_ref[...]), total).astype(BF16)


def attend_kernel(step, tile_len, first, last, qt_ref, bias_ref, same_ref, pair_ref, *refs):
    rows, head_dim = same_ref.shape
    even = lax.axis_index("tensor") % 2 == 0
    keys = jnp.where(even, same_ref[...], pair_ref[...])
    values = jnp.where(even, pair_ref[...], same_ref[...])
    section = lax.axis_index("section") ^ step
    bias = bias_ref[pl.ds((section * rows) // tile_len, 1), :]
    score = jnp.dot(keys, qt_ref[...], preferred_element_type=F32)
    top = jnp.maximum(jnp.max(score, axis=0, keepdims=True) + bias, TOP_FLOOR)
    if not first:
        top_in, sum_in, mixed_in = refs[:3]
        refs = refs[3:]
        top = jnp.maximum(top, top_in[...])
    weights = jnp.exp(score + (bias - top))
    row_sum = jnp.sum(weights, axis=0, keepdims=True)
    mixed = lax.dot_general(
        values, weights.astype(BF16), (((0,), (0,)), ((), ())), preferred_element_type=F32
    )
    if not first:
        scale = jnp.exp(top_in[...] - top)
        row_sum = row_sum + sum_in[...] * scale
        mixed = mixed + mixed_in[...] * scale
    if not last:
        top_out, sum_out, mixed_out = refs
        top_out[...] = top
        sum_out[...] = row_sum
        mixed_out[...] = mixed
        return
    (out,) = refs
    has_any = jnp.max(bias_ref[...], axis=0, keepdims=True) > -1.0
    context = jnp.where(has_any, mixed / jnp.where(has_any, row_sum, 1.0), 0.0)
    tokens = out.shape[0]
    for head in range(out.shape[1] // head_dim):
        out[:, head * head_dim : (head + 1) * head_dim] = context[
            :, head * tokens : (head + 1) * tokens
        ].T.astype(BF16)


def on_device(queries, images, kv_weight, q_gain, k_gain, tile_mask):
    n_section = lax.axis_size("section")
    n_dp = lax.axis_size("dp")
    n_tensor = lax.axis_size("tensor")
    head_dim = q_gain.shape[0]
    tokens, q_width = queries.shape
    rows, features = images.shape[1:]
    tiles = tile_mask.shape[1]
    own_heads = kv_weight.shape[2] // head_dim
    n_pair = n_tensor // 2
    tile_len = rows * n_section // tiles
    assert own_heads * n_dp == n_pair and tile_len % rows == 0
    pairs = tokens * (q_width // head_dim)
    work = 4 * rows * features * kv_weight.shape[2]

    def swap(value, axis, k):
        return lax.ppermute(value, axis, [(i, i ^ k) for i in range(lax.axis_size(axis))])

    others = [swap(kv_weight, "dp", k) for k in range(1, n_dp)]
    halves = [shape_of((own_heads, rows, head_dim))] * 2
    send, keep, x = call(
        own_kernel,
        [*halves, shape_of((rows, features))],
        "own_head",
        [HBM] * 2,
        flops=work,
        size=2 * (images.size + kv_weight.size),
        scratch=[pltpu.VMEM(kv_weight.shape, BF16), pltpu.SemaphoreType.DMA((2, CHUNKS))],
    )(*in_hbm(images, kv_weight))
    qt, bias, gain = call(
        query_kernel,
        [
            shape_of((head_dim, pairs)),
            shape_of((tiles, pairs), F32),
            shape_of((1, head_dim), F32),
        ],
        "queries",
        [HBM] * 4,
        size=2 * queries.size,
        scratch=[
            pltpu.VMEM(queries.shape, BF16),
            pltpu.VMEM((1, head_dim), F32),
            pltpu.VMEM((tiles, tokens), jnp.int32),
            pltpu.SemaphoreType.DMA((4,)),
        ],
    )(*in_hbm(queries, q_gain.reshape(1, -1), k_gain.reshape(1, -1), tile_mask.T))

    kept, arrived = [], []
    for k in range(n_dp):
        if k > 0:
            send, keep = call(
                other_kernel, halves, "other_head", [VMEM] * 2, flops=work
            )(x, others[k - 1])
        outs = [shape_of((rows, head_dim), F32)] + [shape_of((rows, head_dim))] * (n_pair - 1)
        mine, *sends = call(functools.partial(pair_kernel, k), outs, "pair_sum", [VMEM] * 2)(
            keep, swap(send, "tensor", 1)
        )
        kept.append(mine)
        for j, value in enumerate(sends, 1):
            hops = [
                (d * n_tensor + t, d * n_tensor + (t ^ (2 * j)))
                for d in range(n_dp)
                for t in range(n_tensor)
                if ((t // 2) ^ j) // own_heads == d ^ k
            ]
            arrived.append(lax.ppermute(value, ("dp", "tensor"), hops))
    mine = call(
        norm_kernel,
        shape_of((rows, head_dim)),
        "sum_norm",
        [VMEM] * (1 + len(kept) + len(arrived)),
    )(gain, *kept, *arrived)

    same, pair = [mine], [swap(mine, "tensor", 1)]
    for step in range(1, n_section):
        high = 1 << (step.bit_length() - 1)
        same.append(swap(same[step ^ high], "section", high))
    for step in range(1, n_section):
        pair.append(swap(pair[0], "section", 1) if step == 1 else swap(same[step], "tensor", 1))
    state = []
    for step in range(n_section):
        last = step == n_section - 1
        outs = (
            shape_of((tokens, q_width))
            if last
            else [
                shape_of((1, pairs), F32),
                shape_of((1, pairs), F32),
                shape_of((head_dim, pairs), F32),
            ]
        )
        state = call(
            functools.partial(attend_kernel, step, tile_len, step == 0, last),
            outs,
            "attend",
            [VMEM] * (4 + len(state)),
            flops=4 * pairs * rows * head_dim,
            exps=pairs * rows,
        )(qt, bias, same[step], pair[step], *state)
    return state


def solution(mesh):
    in_specs = (
        P(("section", "dp"), "tensor"),
        P("dp", "section", "tensor"),
        P(None, "tensor", "dp"),
        P(),
        P(),
        P(("section", "dp"), None),
    )
    out_specs = P(("section", "dp"), "tensor")
    return jax.shard_map(
        on_device, mesh=mesh, in_specs=in_specs, out_specs=out_specs, check_vma=False
    )
```

time: 27.7 us -> 31.5 us (1.14)
  starting transfers between devices: 8.81 us -> 20.5 us
  waiting for transfers between devices: 13.9 us -> 4.37 us
  Pallas kernels: 4.8 us -> 6.37 us
    ppermute x6 -> x10, waiting for transfers between devices: 13.9 us -> 3.92 us  [swap(): lax.ppermute(value, axis, [(i, i ^ k) for i in range(lax.axis_size(axis))])]
    ppermute x0 -> x2, starting transfers between devices: none -> 5.96 us  [on_device(): arrived.append(lax.ppermute(value, ('dp', 'tensor'), hops))]
    ppermute x6 -> x10, starting transfers between devices: 8.81 us -> 14.5 us  [swap(): lax.ppermute(value, axis, [(i, i ^ k) for i in range(lax.axis_size(axis))])]
    pallas_call x7 -> x10, Pallas kernels: 4.8 us -> 6.37 us  [the longest x4 2.49 us: on_device(): call(functools.partial(attend_kernel, step, tile_len, step == 0, last), o...]
    ppermute x0 -> x2, waiting for transfers between devices: none -> 0.45 us  [on_device(): arrived.append(lax.ppermute(value, ('dp', 'tensor'), hops))]
  transfers between devices with their start and end apart: 6 -> 12, of which waited for: 6 -> 7; matrix products, arithmetic and copies ran while one was open for 0% -> 0% of each run, Pallas kernels for 11% -> 16%
where the time goes in v2:
time: 31.5 us; the launch traced here: 31.3 us
  starting transfers between devices  20.5 us (65%)
  Pallas kernels  6.37 us (20%)
  waiting for transfers between devices  4.37 us (14%)
    ppermute x10, starting transfers between devices, swap(): lax.ppermute(value, axis, [(i, i ^ k) for i in range(lax.axis_size(axis))])  14.5 us
    ppermute x2, starting transfers between devices, on_device(): arrived.append(lax.ppermute(value, ('dp', 'tensor'), hops))  5.96 us
    ppermute x10, waiting for transfers between devices, swap(): lax.ppermute(value, axis, [(i, i ^ k) for i in range(lax.axis_size(axis))])  3.92 us
    pallas_call x4, Pallas kernels, on_device(): call(functools.partial(attend_kernel, step, tile_len, step == 0, last), o...  2.49 us
    pallas_call x1, Pallas kernels, on_device(): call(own_kernel, [*halves, shape_of((rows, features))], 'own_head', [HBM]...  2.03 us
    pallas_call x1, Pallas kernels, on_device(): call(query_kernel, [shape_of((head_dim, pairs)), shape_of((tiles, pairs),...  1.29 us
  transfers between devices with their start and end apart: 12, of which 7 were waited for; matrix products, arithmetic and copies ran while one was open for 0% of the time, Pallas kernels for 16%

profile of v2, /device:TPU:0, one launch (start us, length us, event | category | flops | bytes accessed | tf_op | source)
XLA Modules:
  0.0 31.3 jit_solution(3970106058464211368)
XLA Ops:
  0.0 0.5 %collective-permute-start.1 = (bf16[2,2048,128]{2,1,0:T(8,128)(2,1)}, bf16[2,2048,128]{2,1,0:T(8,128)(2,1)S(1)}, u32[]{:S(2)}, u32[]{:S(2)}) collective-permute-start(bf16[2,2048,128]{2,1,0:T(8,128)(2,1)} %w_hbm.1), channel_id=1, source_target_pairs={{0,4},{4,0},{1,5},{5,1},{2,6},{6,2},{3,7},{7,3},{8,12},{12,8},{9,1... | collective-permute-start | bytes 3145736 | tf_op jit(solution)/shard_map/ppermute | solution.py:196
  0.5 2.0 %own_head.1 = (bf16[1,200,128]{2,1,0:T(8,128)(2,1)S(1)}, bf16[1,200,128]{2,1,0:T(8,128)(2,1)S(1)}, bf16[200,2048]{1,0:T(8,128)(2,1)S(1)}) custom-call(bf16[1,200,2048]{2,1,0:T(8,128)(2,1)} %x_hbm.1, bf16[2,2048,128]{2,1,0:T(8,128)(2,1)} %w_hbm.1), custom_call_target="tpu_custom_call" | custom-call | flops 209715200 | bytes 1867776 | tf_op jit(solution)/shard_map/own_head/pallas_call | solution.py:200
  2.5 2.6 %collective-permute-start = (bf16[1,200,128]{2,1,0:T(8,128)(2,1)S(1)}, bf16[1,200,128]{2,1,0:T(8,128)(2,1)S(1)}, u32[]{:S(2)}, u32[]{:S(2)}) collective-permute-start(bf16[1,200,128]{2,1,0:T(8,128)(2,1)S(1)} %get-tuple-element.30), channel_id=1, source_target_pairs={{0,1},{1,0},{2,3},{3,2},{4,5},{5,4},{6,7},{7,6},{8,9},{9,8},{10,11... | collective-permute-start | bytes 153608 | tf_op jit(solution)/shard_map/ppermute | solution.py:196
  5.1 0.0 collective-permute-done.1.w_ref
  5.1 0.4 %other_head.1 = (bf16[1,200,128]{2,1,0:T(8,128)(2,1)S(1)}, bf16[1,200,128]{2,1,0:T(8,128)(2,1)S(1)}) custom-call(bf16[200,2048]{1,0:T(8,128)(2,1)S(1)} %get-tuple-element.32.x_ref, bf16[2,2048,128]{2,1,0:T(8,128)(2,1)S(1)} %collective-permute-done.1.w_ref), custom_call_target="tpu_custom_call" | custom-call | flops 209715200 | tf_op jit(solution)/shard_map/other_head/pallas_call | solution.py:230
  5.5 0.8 %collective-permute-start.2 = (bf16[1,200,128]{2,1,0:T(8,128)(2,1)S(1)}, bf16[1,200,128]{2,1,0:T(8,128)(2,1)S(1)}, u32[]{:S(2)}, u32[]{:S(2)}) collective-permute-start(bf16[1,200,128]{2,1,0:T(8,128)(2,1)S(1)} %get-tuple-element.34), channel_id=1, source_target_pairs={{0,1},{1,0},{2,3},{3,2},{4,5},{5,4},{6,7},{7,6},{8,9},{9,8},{10,11... | collective-permute-start | bytes 153608 | tf_op jit(solution)/shard_map/ppermute | solution.py:196
  6.4 1.2 %collective-permute-done.arrived_ref = bf16[1,200,128]{2,1,0:T(8,128)(2,1)S(1)} collective-permute-done((bf16[1,200,128]{2,1,0:T(8,128)(2,1)S(1)}, bf16[1,200,128]{2,1,0:T(8,128)(2,1)S(1)}, u32[]{:S(2)}, u32[]{:S(2)}) %collective-permute-start) | collective-permute-done | bytes 51232 | tf_op jit(solution)/shard_map/ppermute | solution.py:196
  7.6 1.3 %collective-permute-start.3 = (bf16[200,128]{1,0:T(8,128)(2,1)S(1)}, bf16[200,128]{1,0:T(8,128)(2,1)S(1)}, u32[]{:S(2)}, u32[]{:S(2)}) collective-permute-start(bf16[200,128]{1,0:T(8,128)(2,1)S(1)} %get-tuple-element.36), channel_id=1, source_target_pairs={{2,0},{3,1},{4,6},{5,7},{10,8},{11,9},{12,14},{13,15},{18,16},{19,... | collective-permute-start | bytes 153608 | tf_op jit(solution)/shard_map/ppermute | solution.py:245
  8.9 0.8 %collective-permute-done.2.arrived_ref = bf16[1,200,128]{2,1,0:T(8,128)(2,1)S(1)} collective-permute-done((bf16[1,200,128]{2,1,0:T(8,128)(2,1)S(1)}, bf16[1,200,128]{2,1,0:T(8,128)(2,1)S(1)}, u32[]{:S(2)}, u32[]{:S(2)}) %collective-permute-start.2) | collective-permute-done | bytes 51232 | tf_op jit(solution)/shard_map/ppermute | solution.py:196
  9.7 4.7 %collective-permute-start.4 = (bf16[200,128]{1,0:T(8,128)(2,1)S(1)}, bf16[200,128]{1,0:T(8,128)(2,1)S(1)}, u32[]{:S(2)}, u32[]{:S(2)}) collective-permute-start(bf16[200,128]{1,0:T(8,128)(2,1)S(1)} %get-tuple-element.37), channel_id=1, source_target_pairs={{0,2},{1,3},{6,4},{7,5},{8,10},{9,11},{14,12},{15,13},{16,18},{17,... | collective-permute-start | bytes 153608 | tf_op jit(solution)/shard_map/ppermute | solution.py:245
  14.4 1.3 %queries.1 = (bf16[128,512]{1,0:T(8,128)(2,1)S(1)}, f32[4,512]{1,0:T(4,128)S(1)}, f32[1,128]{1,0:T(1,128)S(1)}) custom-call(bf16[128,512]{1,0:T(8,128)(2,1)} %q_hbm.1, f32[1,128]{1,0:T(1,128)} %bitcast.4, f32[1,128]{1,0:T(1,128)} %bitcast.5, s32[4,128]{1,0:T(4,128)} %bitcast.3), custom_call_target="tpu_custom_call" | custom-call | bytes 131072 | tf_op jit(solution)/shard_map/queries/pallas_call | solution.py:209
  15.7 0.0 collective-permute-done.3.refs_2_
  15.7 0.4 %collective-permute-done.4.refs_3_ = bf16[200,128]{1,0:T(8,128)(2,1)S(1)} collective-permute-done((bf16[200,128]{1,0:T(8,128)(2,1)S(1)}, bf16[200,128]{1,0:T(8,128)(2,1)S(1)}, u32[]{:S(2)}, u32[]{:S(2)}) %collective-permute-start.4) | collective-permute-done | bytes 51232 | tf_op jit(solution)/shard_map/ppermute | solution.py:245
  16.2 0.1 sum_norm.1.same_ref
  16.3 1.7 %collective-permute-start.5 = (bf16[200,128]{1,0:T(8,128)(2,1)S(1)}, bf16[200,128]{1,0:T(8,128)(2,1)S(1)}, u32[]{:S(2)}, u32[]{:S(2)}) collective-permute-start(bf16[200,128]{1,0:T(8,128)(2,1)S(1)} %sum_norm.1.same_ref), channel_id=1, source_target_pairs={{0,8},{8,0},{16,24},{24,16},{1,9},{9,1},{17,25},{25,17},{2,10},{10... | collective-permute-start | bytes 153608 | tf_op jit(solution)/shard_map/ppermute | solution.py:196
  18.0 1.9 %collective-permute-start.10 = (bf16[200,128]{1,0:T(8,128)(2,1)S(1)}, bf16[200,128]{1,0:T(8,128)(2,1)S(1)}, u32[]{:S(2)}, u32[]{:S(2)}) collective-permute-start(bf16[200,128]{1,0:T(8,128)(2,1)S(1)} %sum_norm.1.same_ref), channel_id=1, source_target_pairs={{0,1},{1,0},{2,3},{3,2},{4,5},{5,4},{6,7},{7,6},{8,9},{9,8},{10,11... | collective-permute-start | bytes 153608 | tf_op jit(solution)/shard_map/ppermute | solution.py:196
  19.9 1.5 %collective-permute-start.8 = (bf16[200,128]{1,0:T(8,128)(2,1)S(1)}, bf16[200,128]{1,0:T(8,128)(2,1)S(1)}, u32[]{:S(2)}, u32[]{:S(2)}) collective-permute-start(bf16[200,128]{1,0:T(8,128)(2,1)S(1)} %sum_norm.1.same_ref), channel_id=1, source_target_pairs={{0,16},{8,24},{16,0},{24,8},{1,17},{9,25},{17,1},{25,9},{2,18},{10... | collective-permute-start | bytes 153608 | tf_op jit(solution)/shard_map/ppermute | solution.py:196
  21.4 0.0 collective-permute-done.5.same_ref
  21.4 1.0 %collective-permute-start.6 = (bf16[200,128]{1,0:T(8,128)(2,1)S(1)}, bf16[200,128]{1,0:T(8,128)(2,1)S(1)}, u32[]{:S(2)}, u32[]{:S(2)}) collective-permute-start(bf16[200,128]{1,0:T(8,128)(2,1)S(1)} %collective-permute-done.5.same_ref), channel_id=1, source_target_pairs={{0,16},{8,24},{16,0},{24,8},{1,17},{9,25},{17,1},{25,9},{2,18},{10... | collective-permute-start | bytes 153608 | tf_op jit(solution)/shard_map/ppermute | solution.py:196
  22.5 0.2 collective-permute-done.10.pair_ref
  22.6 1.3 %collective-permute-start.11 = (bf16[200,128]{1,0:T(8,128)(2,1)S(1)}, bf16[200,128]{1,0:T(8,128)(2,1)S(1)}, u32[]{:S(2)}, u32[]{:S(2)}) collective-permute-start(bf16[200,128]{1,0:T(8,128)(2,1)S(1)} %collective-permute-done.10.pair_ref), channel_id=1, source_target_pairs={{0,8},{8,0},{16,24},{24,16},{1,9},{9,1},{17,25},{25,17},{2,10},{10... | collective-permute-start | bytes 153608 | tf_op jit(solution)/shard_map/ppermute | solution.py:196
  24.0 0.1 collective-permute-done.8.same_ref
  24.0 2.0 %collective-permute-start.9 = (bf16[200,128]{1,0:T(8,128)(2,1)S(1)}, bf16[200,128]{1,0:T(8,128)(2,1)S(1)}, u32[]{:S(2)}, u32[]{:S(2)}) collective-permute-start(bf16[200,128]{1,0:T(8,128)(2,1)S(1)} %collective-permute-done.8.same_ref), channel_id=1, source_target_pairs={{0,1},{1,0},{2,3},{3,2},{4,5},{5,4},{6,7},{7,6},{8,9},{9,8},{10,11... | collective-permute-start | bytes 153608 | tf_op jit(solution)/shard_map/ppermute | solution.py:196
  26.0 0.0 collective-permute-done.6.same_ref
  26.0 1.1 %collective-permute-start.7 = (bf16[200,128]{1,0:T(8,128)(2,1)S(1)}, bf16[200,128]{1,0:T(8,128)(2,1)S(1)}, u32[]{:S(2)}, u32[]{:S(2)}) collective-permute-start(bf16[200,128]{1,0:T(8,128)(2,1)S(1)} %collective-permute-done.6.same_ref), channel_id=1, source_target_pairs={{0,1},{1,0},{2,3},{3,2},{4,5},{5,4},{6,7},{7,6},{8,9},{9,8},{10,11... | collective-permute-start | bytes 153608 | tf_op jit(solution)/shard_map/ppermute | solution.py:196
  27.1 0.4 %attend.4 = (f32[1,512]{1,0:T(1,128)S(1)}, f32[1,512]{1,0:T(1,128)S(1)}, f32[128,512]{1,0:T(8,128)S(1)}) custom-call(bf16[128,512]{1,0:T(8,128)(2,1)S(1)} %get-tuple-element.26.qt_ref, f32[4,512]{1,0:T(4,128)S(1)} %get-tuple-element.27.bias_ref, bf16[200,128]{1,0:T(8,128)(2,1)S(1)} %sum_norm.1.same_ref, bf16[200,128]{1,0:T(8,128)(2,1)S(1)} %collective-permute-done.10.pair_ref), custom_call_target="tpu_custom_call" | custom-call | flops 52428800 | tf_op jit(solution)/shard_map/attend/pallas_call | solution.py:271
  27.5 0.0 collective-permute-done.11.pair_ref
  27.6 0.4 %attend.5 = (f32[1,512]{1,0:T(1,128)S(1)}, f32[1,512]{1,0:T(1,128)S(1)}, f32[128,512]{1,0:T(8,128)S(1)}) custom-call(bf16[128,512]{1,0:T(8,128)(2,1)S(1)} %get-tuple-element.26.qt_ref, f32[4,512]{1,0:T(4,128)S(1)} %get-tuple-element.27.bias_ref, bf16[200,128]{1,0:T(8,128)(2,1)S(1)} %collective-permute-done.5.same_ref, ...), custom_call_target="tpu_custom_call" | custom-call | flops 52428800 | tf_op jit(solution)/shard_map/attend/pallas_call | solution.py:271
  28.0 0.5 %collective-permute-done.9.pair_ref = bf16[200,128]{1,0:T(8,128)(2,1)S(1)} collective-permute-done((bf16[200,128]{1,0:T(8,128)(2,1)S(1)}, bf16[200,128]{1,0:T(8,128)(2,1)S(1)}, u32[]{:S(2)}, u32[]{:S(2)}) %collective-permute-start.9) | collective-permute-done | bytes 51232 | tf_op jit(solution)/shard_map/ppermute | solution.py:196
  28.5 0.4 %attend.6 = (f32[1,512]{1,0:T(1,128)S(1)}, f32[1,512]{1,0:T(1,128)S(1)}, f32[128,512]{1,0:T(8,128)S(1)}) custom-call(bf16[128,512]{1,0:T(8,128)(2,1)S(1)} %get-tuple-element.26.qt_ref, f32[4,512]{1,0:T(4,128)S(1)} %get-tuple-element.27.bias_ref, bf16[200,128]{1,0:T(8,128)(2,1)S(1)} %collective-permute-done.8.same_ref, ...), custom_call_target="tpu_custom_call" | custom-call | flops 52428800 | tf_op jit(solution)/shard_map/attend/pallas_call | solution.py:271
  28.9 1.2 %collective-permute-done.7.pair_ref = bf16[200,128]{1,0:T(8,128)(2,1)S(1)} collective-permute-done((bf16[200,128]{1,0:T(8,128)(2,1)S(1)}, bf16[200,128]{1,0:T(8,128)(2,1)S(1)}, u32[]{:S(2)}, u32[]{:S(2)}) %collective-permute-start.7) | collective-permute-done | bytes 51232 | tf_op jit(solution)/shard_map/ppermute | solution.py:196
  30.1 1.2 %attend.7 = bf16[128,512]{1,0:T(8,128)(2,1)} custom-call(bf16[128,512]{1,0:T(8,128)(2,1)S(1)} %get-tuple-element.26.qt_ref, f32[4,512]{1,0:T(4,128)S(1)} %get-tuple-element.27.bias_ref, bf16[200,128]{1,0:T(8,128)(2,1)S(1)} %collective-permute-done.6.same_ref, bf16[200,128]{1,0:T(8,128)(2,1)S(1)} %collective-permute-done.7.pair_ref, ...), custom_call_target="tpu_custom_call" | custom-call | flops 52428800 | tf_op jit(solution)/shard_map/attend/pallas_call | solution.py:271
  (2 shorter events, 0.0 us)
Async XLA Ops:
  0.0 5.1 %collective-permute-start.1 = (bf16[2,2048,128]{2,1,0:T(8,128)(2,1)}, bf16[2,2048,128]{2,1,0:T(8,128)(2,1)S(1)}, u32[]{:S(2)}, u32[]{:S(2)}) collective-permute-start(bf16[2,2048,128]{2,1,0:T(8,128)(2,1)} %w_hbm.1), channel_id=1, source_target_pairs={{0,4},{4,0},{1,5},{5,1},{2,6},{6,2},{3,7},{7,3},{8,12},{12,8},{9,1... | collective-permute-start | bytes 3145736 | tf_op jit(solution)/shard_map/ppermute | solution.py:196
  2.5 5.1 %collective-permute-start = (bf16[1,200,128]{2,1,0:T(8,128)(2,1)S(1)}, bf16[1,200,128]{2,1,0:T(8,128)(2,1)S(1)}, u32[]{:S(2)}, u32[]{:S(2)}) collective-permute-start(bf16[1,200,128]{2,1,0:T(8,128)(2,1)S(1)} %get-tuple-element.30), channel_id=1, source_target_pairs={{0,1},{1,0},{2,3},{3,2},{4,5},{5,4},{6,7},{7,6},{8,9},{9,8},{10,11... | collective-permute-start | bytes 153608 | tf_op jit(solution)/shard_map/ppermute | solution.py:196
  5.5 4.2 %collective-permute-start.2 = (bf16[1,200,128]{2,1,0:T(8,128)(2,1)S(1)}, bf16[1,200,128]{2,1,0:T(8,128)(2,1)S(1)}, u32[]{:S(2)}, u32[]{:S(2)}) collective-permute-start(bf16[1,200,128]{2,1,0:T(8,128)(2,1)S(1)} %get-tuple-element.34), channel_id=1, source_target_pairs={{0,1},{1,0},{2,3},{3,2},{4,5},{5,4},{6,7},{7,6},{8,9},{9,8},{10,11... | collective-permute-start | bytes 153608 | tf_op jit(solution)/shard_map/ppermute | solution.py:196
  7.6 8.1 %collective-permute-start.3 = (bf16[200,128]{1,0:T(8,128)(2,1)S(1)}, bf16[200,128]{1,0:T(8,128)(2,1)S(1)}, u32[]{:S(2)}, u32[]{:S(2)}) collective-permute-start(bf16[200,128]{1,0:T(8,128)(2,1)S(1)} %get-tuple-element.36), channel_id=1, source_target_pairs={{2,0},{3,1},{4,6},{5,7},{10,8},{11,9},{12,14},{13,15},{18,16},{19,... | collective-permute-start | bytes 153608 | tf_op jit(solution)/shard_map/ppermute | solution.py:245
  9.7 6.4 %collective-permute-start.4 = (bf16[200,128]{1,0:T(8,128)(2,1)S(1)}, bf16[200,128]{1,0:T(8,128)(2,1)S(1)}, u32[]{:S(2)}, u32[]{:S(2)}) collective-permute-start(bf16[200,128]{1,0:T(8,128)(2,1)S(1)} %get-tuple-element.37), channel_id=1, source_target_pairs={{0,2},{1,3},{6,4},{7,5},{8,10},{9,11},{14,12},{15,13},{16,18},{17,... | collective-permute-start | bytes 153608 | tf_op jit(solution)/shard_map/ppermute | solution.py:245
  16.3 5.1 %collective-permute-start.5 = (bf16[200,128]{1,0:T(8,128)(2,1)S(1)}, bf16[200,128]{1,0:T(8,128)(2,1)S(1)}, u32[]{:S(2)}, u32[]{:S(2)}) collective-permute-start(bf16[200,128]{1,0:T(8,128)(2,1)S(1)} %sum_norm.1.same_ref), channel_id=1, source_target_pairs={{0,8},{8,0},{16,24},{24,16},{1,9},{9,1},{17,25},{25,17},{2,10},{10... | collective-permute-start | bytes 153608 | tf_op jit(solution)/shard_map/ppermute | solution.py:196
  18.0 4.6 %collective-permute-start.10 = (bf16[200,128]{1,0:T(8,128)(2,1)S(1)}, bf16[200,128]{1,0:T(8,128)(2,1)S(1)}, u32[]{:S(2)}, u32[]{:S(2)}) collective-permute-start(bf16[200,128]{1,0:T(8,128)(2,1)S(1)} %sum_norm.1.same_ref), channel_id=1, source_target_pairs={{0,1},{1,0},{2,3},{3,2},{4,5},{5,4},{6,7},{7,6},{8,9},{9,8},{10,11... | collective-permute-start | bytes 153608 | tf_op jit(solution)/shard_map/ppermute | solution.py:196
  19.9 4.1 %collective-permute-start.8 = (bf16[200,128]{1,0:T(8,128)(2,1)S(1)}, bf16[200,128]{1,0:T(8,128)(2,1)S(1)}, u32[]{:S(2)}, u32[]{:S(2)}) collective-permute-start(bf16[200,128]{1,0:T(8,128)(2,1)S(1)} %sum_norm.1.same_ref), channel_id=1, source_target_pairs={{0,16},{8,24},{16,0},{24,8},{1,17},{9,25},{17,1},{25,9},{2,18},{10... | collective-permute-start | bytes 153608 | tf_op jit(solution)/shard_map/ppermute | solution.py:196
  21.4 4.6 %collective-permute-start.6 = (bf16[200,128]{1,0:T(8,128)(2,1)S(1)}, bf16[200,128]{1,0:T(8,128)(2,1)S(1)}, u32[]{:S(2)}, u32[]{:S(2)}) collective-permute-start(bf16[200,128]{1,0:T(8,128)(2,1)S(1)} %collective-permute-done.5.same_ref), channel_id=1, source_target_pairs={{0,16},{8,24},{16,0},{24,8},{1,17},{9,25},{17,1},{25,9},{2,18},{10... | collective-permute-start | bytes 153608 | tf_op jit(solution)/shard_map/ppermute | solution.py:196
  22.6 4.9 %collective-permute-start.11 = (bf16[200,128]{1,0:T(8,128)(2,1)S(1)}, bf16[200,128]{1,0:T(8,128)(2,1)S(1)}, u32[]{:S(2)}, u32[]{:S(2)}) collective-permute-start(bf16[200,128]{1,0:T(8,128)(2,1)S(1)} %collective-permute-done.10.pair_ref), channel_id=1, source_target_pairs={{0,8},{8,0},{16,24},{24,16},{1,9},{9,1},{17,25},{25,17},{2,10},{10... | collective-permute-start | bytes 153608 | tf_op jit(solution)/shard_map/ppermute | solution.py:196
  24.0 4.5 %collective-permute-start.9 = (bf16[200,128]{1,0:T(8,128)(2,1)S(1)}, bf16[200,128]{1,0:T(8,128)(2,1)S(1)}, u32[]{:S(2)}, u32[]{:S(2)}) collective-permute-start(bf16[200,128]{1,0:T(8,128)(2,1)S(1)} %collective-permute-done.8.same_ref), channel_id=1, source_target_pairs={{0,1},{1,0},{2,3},{3,2},{4,5},{5,4},{6,7},{7,6},{8,9},{9,8},{10,11... | collective-permute-start | bytes 153608 | tf_op jit(solution)/shard_map/ppermute | solution.py:196
  26.0 4.1 %collective-permute-start.7 = (bf16[200,128]{1,0:T(8,128)(2,1)S(1)}, bf16[200,128]{1,0:T(8,128)(2,1)S(1)}, u32[]{:S(2)}, u32[]{:S(2)}) collective-permute-start(bf16[200,128]{1,0:T(8,128)(2,1)S(1)} %collective-permute-done.6.same_ref), channel_id=1, source_target_pairs={{0,1},{1,0},{2,3},{3,2},{4,5},{5,4},{6,7},{7,6},{8,9},{9,8},{10,11... | collective-permute-start | bytes 153608 | tf_op jit(solution)/shard_map/ppermute | solution.py:196

commit v3 on v2

v3 whole, which is shorter than its diff:
```python
import functools

import jax
import jax.numpy as jnp
from jax import lax
from jax.experimental import pallas as pl
from jax.experimental.pallas import tpu as pltpu
from jax.sharding import PartitionSpec as P

EPSILON = 1e-05
MASKED_SCORE = -1e30
TOP_FLOOR = -1e29
VMEM = pl.BlockSpec(memory_space=pltpu.VMEM)
HBM = pl.BlockSpec(memory_space=pltpu.HBM)
F32 = jnp.float32
BF16 = jnp.bfloat16
LIMIT = 24 * 1024 * 1024
CHUNKS = 4


def shape_of(dims, dtype=BF16):
    return jax.ShapeDtypeStruct(dims, dtype)


def call(kernel, outs, name, in_specs, flops=0, size=0, exps=0, scratch=()):
    many = isinstance(outs, list)
    return pl.pallas_call(
        kernel,
        out_shape=outs,
        in_specs=in_specs,
        out_specs=[VMEM] * len(outs) if many else VMEM,
        scratch_shapes=scratch,
        compiler_params=pltpu.CompilerParams(vmem_limit_bytes=LIMIT),
        cost_estimate=pl.CostEstimate(flops=flops, bytes_accessed=size, transcendentals=exps),
        name=name,
    )


def in_hbm(*values):
    return [pltpu.with_memory_space_constraint(value, pltpu.HBM) for value in values]


def normalize(values, gain_vec):
    mean_sq = jnp.mean(values * values, axis=-1, keepdims=True)
    return values * lax.rsqrt(mean_sq + EPSILON) * gain_vec


def store_heads(ref, base, both, head_dim):
    width = both.shape[1] // 2
    both = both.astype(BF16)
    for head in range(width // head_dim):
        lo = head * head_dim
        ref[base + 2 * head] = both[:, lo : lo + head_dim]
        ref[base + 2 * head + 1] = both[:, width + lo : width + lo + head_dim]


def own_kernel(x_hbm, w_hbm, own_ref, x_ref, w_ref, sems):
    step = x_ref.shape[1] // CHUNKS
    copies = []
    for i in range(CHUNKS):
        cols = pl.ds(i * step, step)
        copies.append(
            (
                pltpu.make_async_copy(w_hbm.at[:, cols], w_ref.at[:, cols], sems.at[0, i]),
                pltpu.make_async_copy(x_hbm.at[0, :, cols], x_ref.at[:, cols], sems.at[1, i]),
            )
        )
        for copy in copies[-1]:
            copy.start()
    both = None
    for i in range(CHUNKS):
        for copy in copies[i]:
            copy.wait()
        cols = slice(i * step, (i + 1) * step)
        part = jnp.dot(
            x_ref[:, cols],
            jnp.concatenate([w_ref[0, cols], w_ref[1, cols]], axis=1),
            preferred_element_type=F32,
        )
        both = part if both is None else both + part
    store_heads(own_ref, 0, both, own_ref.shape[2])


def other_kernel(x_ref, own_ref, *refs):
    w_refs, parts_ref = refs[:-1], refs[-1]
    pieces = own_ref.shape[0]
    d = lax.axis_index("dp")
    parts_ref[pl.ds(d * pieces, pieces)] = own_ref[...]
    for k, w_ref in enumerate(w_refs, 1):
        both = jnp.dot(
            x_ref[...],
            jnp.concatenate([w_ref[0], w_ref[1]], axis=1),
            preferred_element_type=F32,
        )
        store_heads(parts_ref, (d ^ k) * pieces, both, own_ref.shape[2])


def query_kernel(
    q_hbm, q_gain_hbm, k_gain_hbm, mask_hbm, qt_ref, bias_ref, k_gain_ref,
    q_ref, q_gain_ref, mask_ref, sems,
):
    moves = [
        (q_hbm, q_ref),
        (q_gain_hbm, q_gain_ref),
        (mask_hbm, mask_ref),
        (k_gain_hbm, k_gain_ref),
    ]
    copies = [pltpu.make_async_copy(a, b, sems.at[i]) for i, (a, b) in enumerate(moves)]
    for copy in copies:
        copy.start()
    for copy in copies:
        copy.wait()
    tokens = q_ref.shape[0]
    head_dim = q_gain_ref.shape[1]
    bias = jnp.where(mask_ref[...] > 0, 0.0, MASKED_SCORE).astype(F32)
    for head in range(q_ref.shape[1] // head_dim):
        rows = q_ref[:, head * head_dim : (head + 1) * head_dim].astype(F32)
        normed = normalize(rows, q_gain_ref[...]) * head_dim ** (-0.5)
        qt_ref[:, head * tokens : (head + 1) * tokens] = normed.T.astype(BF16)
        bias_ref[:, head * tokens : (head + 1) * tokens] = bias


def norm_kernel(k_gain_ref, parts_ref, out_ref):
    total = parts_ref[0].astype(F32)
    for i in range(1, parts_ref.shape[0]):
        total = total + parts_ref[i].astype(F32)
    is_key = lax.axis_index("kind") == 0
    total = jnp.where(is_key, normalize(total, k_gain_ref[...]), total).astype(BF16)
    for i in range(out_ref.shape[0]):
        out_ref[i] = total


def attend_kernel(tile_len, qt_ref, bias_ref, kv_ref, out_ref):
    n_section = kv_ref.shape[0] // 2
    rows, head_dim = kv_ref.shape[1:]
    qt = qt_ref[...]
    scores, biases = [], []
    top = TOP_FLOOR
    for section in range(n_section):
        score = jnp.dot(kv_ref[2 * section], qt, preferred_element_type=F32)
        tile = section * rows // tile_len
        bias = bias_ref[tile : tile + 1, :]
        scores.append(score)
        biases.append(bias)
        top = jnp.maximum(top, jnp.max(score, axis=0, keepdims=True) + bias)
    row_sum, mixed = 0.0, 0.0
    for section in range(n_section):
        weights = jnp.exp(scores[section] + (biases[section] - top))
        row_sum = row_sum + jnp.sum(weights, axis=0, keepdims=True)
        mixed = mixed + lax.dot_general(
            kv_ref[2 * section + 1],
            weights.astype(BF16),
            (((0,), (0,)), ((), ())),
            preferred_element_type=F32,
        )
    has_any = jnp.max(bias_ref[...], axis=0, keepdims=True) > -1.0
    context = jnp.where(has_any, mixed / jnp.where(has_any, row_sum, 1.0), 0.0)
    tokens = out_ref.shape[0]
    for head in range(out_ref.shape[1] // head_dim):
        out_ref[:, head * head_dim : (head + 1) * head_dim] = context[
            :, head * tokens : (head + 1) * tokens
        ].T.astype(BF16)


def on_device(queries, images, kv_weight, q_gain, k_gain, tile_mask):
    n_section = lax.axis_size("section")
    n_dp = lax.axis_size("dp")
    n_tensor = lax.axis_size("pair") * lax.axis_size("kind")
    head_dim = q_gain.shape[0]
    tokens, q_width = queries.shape
    rows, features = images.shape[1:]
    tiles = tile_mask.shape[1]
    own_heads = kv_weight.shape[2] // head_dim
    tile_len = rows * n_section // tiles
    assert 2 * own_heads * n_dp == n_tensor and tile_len % rows == 0
    pairs = tokens * (q_width // head_dim)
    work = 4 * rows * features * kv_weight.shape[2]

    n_kind = lax.axis_size("kind")
    pieces = 2 * own_heads

    others = [
        lax.ppermute(kv_weight, "dp", [(i, i ^ k) for i in range(n_dp)]) for k in range(1, n_dp)
    ]
    own, x = call(
        own_kernel,
        [shape_of((pieces, rows, head_dim)), shape_of((rows, features))],
        "own_head",
        [HBM] * 2,
        flops=work,
        size=2 * (images.size + kv_weight.size),
        scratch=[pltpu.VMEM(kv_weight.shape, BF16), pltpu.SemaphoreType.DMA((2, CHUNKS))],
    )(*in_hbm(images, kv_weight))
    qt, bias, gain = call(
        query_kernel,
        [
            shape_of((head_dim, pairs)),
            shape_of((tiles, pairs), F32),
            shape_of((1, head_dim), F32),
        ],
        "queries",
        [HBM] * 4,
        size=2 * queries.size,
        scratch=[
            pltpu.VMEM(queries.shape, BF16),
            pltpu.VMEM((1, head_dim), F32),
            pltpu.VMEM((tiles, tokens), jnp.int32),
            pltpu.SemaphoreType.DMA((4,)),
        ],
    )(*in_hbm(queries, q_gain.reshape(1, -1), k_gain.reshape(1, -1), tile_mask.T))

    parts = call(
        other_kernel,
        shape_of((n_tensor, rows, head_dim)),
        "other_heads",
        [VMEM] * (n_dp + 1),
        flops=work * (n_dp - 1),
    )(x, own, *others)
    parts = lax.all_to_all(parts, ("pair", "kind"), 0, 0, tiled=True)
    copies = call(
        norm_kernel, shape_of((n_section * n_kind, rows, head_dim)), "sum_norm", [VMEM] * 2
    )(gain, parts)
    kv = lax.all_to_all(copies, ("section", "kind"), 0, 0, tiled=True)
    return call(
        functools.partial(attend_kernel, tile_len),
        shape_of((tokens, q_width)),
        "attend",
        [VMEM] * 3,
        flops=4 * pairs * rows * head_dim * n_section,
        exps=pairs * rows * n_section,
    )(qt, bias, kv)


def solution(mesh):
    sizes = mesh.shape
    mesh = jax.sharding.Mesh(
        mesh.devices.reshape(sizes["section"], sizes["dp"], sizes["tensor"] // 2, 2),
        ("section", "dp", "pair", "kind"),
    )
    tensor = ("pair", "kind")
    in_specs = (
        P(("section", "dp"), tensor),
        P("dp", "section", tensor),
        P(None, tensor, "dp"),
        P(),
        P(),
        P(("section", "dp"), None),
    )
    out_specs = P(("section", "dp"), tensor)
    return jax.shard_map(
        on_device, mesh=mesh, in_specs=in_specs, out_specs=out_specs, check_vma=False
    )
```

time: 31.5 us -> 31.5 us (level)
  starting transfers between devices: 20.5 us -> 6.69 us
  blocking collectives: 0 us -> 11.3 us
  waiting for transfers between devices: 4.37 us -> 7.16 us
    ppermute x12 -> x1, starting transfers between devices: 20.5 us -> 0.45 us  [on_device(): lax.ppermute(kv_weight, 'dp', [(i, i ^ k) for i in range(n_dp)])]
    all_to_all x0 -> x1, blocking collectives: none -> 11.3 us  [on_device(): kv = lax.all_to_all(copies, ('section', 'kind'), 0, 0, tiled=True)]
    all_to_all x0 -> x1, waiting for transfers between devices: none -> 6.7 us  [on_device(): parts = lax.all_to_all(parts, ('pair', 'kind'), 0, 0, tiled=True)]
    all_to_all x0 -> x1, starting transfers between devices: none -> 6.24 us  [on_device(): parts = lax.all_to_all(parts, ('pair', 'kind'), 0, 0, tiled=True)]
    ppermute x12 -> x1, waiting for transfers between devices: 4.37 us -> 0.46 us  [on_device(): lax.ppermute(kv_weight, 'dp', [(i, i ^ k) for i in range(n_dp)])]
    pallas_call x9 -> x4, Pallas kernels: 5.08 us -> 4.83 us  [the longest x1 2.03 us: on_device(): call(own_kernel, [shape_of((pieces, rows, head_dim)), shape_of((rows, fea...]
  transfers between devices with their start and end apart: 12 -> 2, of which waited for: 7 -> 2; matrix products, arithmetic and copies ran while one was open for 0% -> 0% of each run, Pallas kernels for 16% -> 11%
where the time goes in v3:
time: 31.5 us; the launch traced here: 31.3 us
  blocking collectives  11.3 us (36%)
  waiting for transfers between devices  7.16 us (23%)
  starting transfers between devices  6.69 us (21%)
  Pallas kernels  6.11 us (19%)
    all_to_all x1, blocking collectives, on_device(): kv = lax.all_to_all(copies, ('section', 'kind'), 0, 0, tiled=True)  11.3 us
    all_to_all x1, waiting for transfers between devices, on_device(): parts = lax.all_to_all(parts, ('pair', 'kind'), 0, 0, tiled=True)  6.7 us
    all_to_all x1, starting transfers between devices, on_device(): parts = lax.all_to_all(parts, ('pair', 'kind'), 0, 0, tiled=True)  6.24 us
    pallas_call x1, Pallas kernels, on_device(): call(own_kernel, [shape_of((pieces, rows, head_dim)), shape_of((rows, fea...  2.03 us
    pallas_call x1, Pallas kernels, on_device(): call(functools.partial(attend_kernel, tile_len), shape_of((tokens, q_widt...  1.6 us
    pallas_call x1, Pallas kernels, on_device(): call(query_kernel, [shape_of((head_dim, pairs)), shape_of((tiles, pairs),...  1.28 us
    pallas_call x1, Pallas kernels, on_device(): call(other_kernel, shape_of((n_tensor, rows, head_dim)), 'other_heads', [...  1.08 us
  transfers between devices with their start and end apart: 2, of which 2 were waited for; matrix products, arithmetic and copies ran while one was open for 0% of the time, Pallas kernels for 11%

profile of v3, /device:TPU:0, one launch (start us, length us, event | category | flops | bytes accessed | tf_op | source)
XLA Modules:
  0.0 31.3 jit_solution(17904608877737279588)
XLA Ops:
  0.0 0.5 %collective-permute-start = (bf16[2,2048,128]{2,1,0:T(8,128)(2,1)}, bf16[2,2048,128]{2,1,0:T(8,128)(2,1)S(1)}, u32[]{:S(2)}, u32[]{:S(2)}) collective-permute-start(bf16[2,2048,128]{2,1,0:T(8,128)(2,1)} %w_hbm.1), channel_id=1, source_target_pairs={{0,4},{4,0},{1,5},{5,1},{2,6},{6,2},{3,7},{7,3},{8,12},{12,8},{9,1... | collective-permute-start | bytes 3145736 | tf_op jit(solution)/shard_map/ppermute | solution.py:183
  0.5 2.0 %own_head.1 = (bf16[2,200,128]{2,1,0:T(8,128)(2,1)S(1)}, bf16[200,2048]{1,0:T(8,128)(2,1)S(1)}) custom-call(bf16[1,200,2048]{2,1,0:T(8,128)(2,1)} %x_hbm.1, bf16[2,2048,128]{2,1,0:T(8,128)(2,1)} %w_hbm.1), custom_call_target="tpu_custom_call" | custom-call | flops 209715200 | bytes 1867776 | tf_op jit(solution)/shard_map/own_head/pallas_call | solution.py:185
  2.5 0.5 %collective-permute-done.refs_0_ = bf16[2,2048,128]{2,1,0:T(8,128)(2,1)S(1)} collective-permute-done((bf16[2,2048,128]{2,1,0:T(8,128)(2,1)}, bf16[2,2048,128]{2,1,0:T(8,128)(2,1)S(1)}, u32[]{:S(2)}, u32[]{:S(2)}) %collective-permute-start) | collective-permute-done | bytes 1048608 | tf_op jit(solution)/shard_map/ppermute | solution.py:183
  3.0 1.1 %other_heads.1 = bf16[4,200,128]{2,1,0:T(8,128)(2,1)} custom-call(bf16[200,2048]{1,0:T(8,128)(2,1)S(1)} %get-tuple-element.13.x_ref, bf16[2,200,128]{2,1,0:T(8,128)(2,1)S(1)} %get-tuple-element.14.own_ref, bf16[2,2048,128]{2,1,0:T(8,128)(2,1)S(1)} %collective-permute-done.refs_0_), custom_call_target="tpu_custom_call" | custom-call | flops 209715200 | tf_op jit(solution)/shard_map/other_heads/pallas_call | solution.py:212
  4.0 6.2 %all-to-all-start = ((bf16[4,200,128]{2,1,0:T(8,128)(2,1)}), bf16[4,200,128]{2,1,0:T(8,128)(2,1)S(1)}, u32[]{:S(2)}, u32[]{:S(2)}) async-start(bf16[4,200,128]{2,1,0:T(8,128)(2,1)} %other_heads.1), calls=%async_computation | async-start | bytes 409600 | tf_op jit(solution)/shard_map/all_to_all | solution.py:219
  10.3 1.3 %queries.1 = (bf16[128,512]{1,0:T(8,128)(2,1)S(1)}, f32[4,512]{1,0:T(4,128)S(1)}, f32[1,128]{1,0:T(1,128)S(1)}) custom-call(bf16[128,512]{1,0:T(8,128)(2,1)} %q_hbm.1, f32[1,128]{1,0:T(1,128)} %bitcast.4, f32[1,128]{1,0:T(1,128)} %bitcast.5, s32[4,128]{1,0:T(4,128)} %bitcast.3), custom_call_target="tpu_custom_call" | custom-call | bytes 131072 | tf_op jit(solution)/shard_map/queries/pallas_call | solution.py:194
  11.6 6.7 %all-to-all-done.parts_ref = bf16[4,200,128]{2,1,0:T(8,128)(2,1)S(1)} async-done(((bf16[4,200,128]{2,1,0:T(8,128)(2,1)}), bf16[4,200,128]{2,1,0:T(8,128)(2,1)S(1)}, u32[]{:S(2)}, u32[]{:S(2)}) %all-to-all-start) | async-done | bytes 204832 | tf_op jit(solution)/shard_map/all_to_all | solution.py:219
  18.3 0.1 sum_norm.1
  18.4 11.3 %all_to_all.10.kv_ref = bf16[8,200,128]{2,1,0:T(8,128)(2,1)S(1)} all-to-all(bf16[8,200,128]{2,1,0:T(8,128)(2,1)S(1)} %sum_norm.1), channel_id=1, replica_groups=mesh['section'=4,'dp'=2,'pair'=2,'kind'=2] {'section','kind'}, dimensions={0} | all-to-all | bytes 819200 | tf_op jit(solution)/shard_map/all_to_all | solution.py:223
  29.7 1.6 %attend.1 = bf16[128,512]{1,0:T(8,128)(2,1)} custom-call(bf16[128,512]{1,0:T(8,128)(2,1)S(1)} %get-tuple-element.10.qt_ref, f32[4,512]{1,0:T(4,128)S(1)} %get-tuple-element.11.bias_ref, bf16[8,200,128]{2,1,0:T(8,128)(2,1)S(1)} %all_to_all.10.kv_ref), custom_call_target="tpu_custom_call" | custom-call | flops 209715200 | tf_op jit(solution)/shard_map/attend/pallas_call | solution.py:224
Async XLA Ops:
  0.0 3.0 %collective-permute-start = (bf16[2,2048,128]{2,1,0:T(8,128)(2,1)}, bf16[2,2048,128]{2,1,0:T(8,128)(2,1)S(1)}, u32[]{:S(2)}, u32[]{:S(2)}) collective-permute-start(bf16[2,2048,128]{2,1,0:T(8,128)(2,1)} %w_hbm.1), channel_id=1, source_target_pairs={{0,4},{4,0},{1,5},{5,1},{2,6},{6,2},{3,7},{7,3},{8,12},{12,8},{9,1... | collective-permute-start | bytes 3145736 | tf_op jit(solution)/shard_map/ppermute | solution.py:183
  4.0 14.2 %all-to-all-start = ((bf16[4,200,128]{2,1,0:T(8,128)(2,1)}), bf16[4,200,128]{2,1,0:T(8,128)(2,1)S(1)}, u32[]{:S(2)}, u32[]{:S(2)}) async-start(bf16[4,200,128]{2,1,0:T(8,128)(2,1)} %other_heads.1), calls=%async_computation | async-start | bytes 409600 | tf_op jit(solution)/shard_map/all_to_all | solution.py:219
